TPU v7x, 256 devices: a whole 4x4x8 slice. The times are simulated.
256 devices in a mesh: phase: 2 (over z_hi), seq: 16 (over z_lo, x), head: 8 (over y, core).
Axes of the slice: x: 4, y: 4, z: 8 (z_hi: 2, z_lo: 4; z = z_hi * 4 + z_lo), core: 2. Of those that a mesh axis runs over, the one named last changes fastest.
Arguments:
- query_feats: bfloat16 [8192, 1024], P('seq', 'head'), may hold values from -4 to 4
- key_feats: bfloat16 [8192, 1024], P('seq', 'head'), may hold values from -4 to 4
- values: bfloat16 [8192, 8192], P('seq', 'head'), may hold values from -6 to 6
- keys_soft: bfloat16 [8192, 1024], P('seq', 'head'), may hold values from -320 to 320
- values_soft: bfloat16 [8192, 1024], P('seq', 'head'), may hold values from -6 to 6
- norm_gain: float32 [8192], P('head'), may hold values from 0.1 to 1.9
- doc_ids: int32 [8192], replicated, may hold values from 0 to 2, never falling along the last dimension, each value on 1 to 4096 neighbouring positions
Outputs:
- mixed: bfloat16 [2, 8192, 8192], P('phase', 'seq', 'head')
Inputs may be any that keep to these rules, and one draw needn't show every extreme that they name: `doc_ids`: non-decreasing along the sequence; each document holds 1 to 4096 positions, and one holds exactly 4096.
All inputs are finite; a program needn't handle non-finite values.
Results may differ from a plain program's by a relative error of at most 0.01.
Values may be sent and summed in bfloat16 or wider, within the bound.
No kernel may reach another device: no remote copies, remote signals or barrier semaphores. Data moves between devices by JAX's collectives and lax.ppermute only.
A program may use at most 320 MiB of HBM per device.

v0:
```python
import math

import jax
import jax.numpy as jnp
from jax import lax
from jax.sharding import PartitionSpec as P

DH = 128
F = 16


precise = lax.Precision.HIGHEST
root_half = 0.5**0.5
far_below = -1e30


def from_behind(x, axis, by):
    length = lax.axis_size(axis)
    pairs = [(i, i + by) for i in range(length) if 0 <= i + by < length]
    return lax.ppermute(x, axis, pairs)


def taylor(vector):
    paired = (vector[..., :, None] * vector[..., None, :]).reshape(
        vector.shape[:-1] + (vector.shape[-1] * vector.shape[-1],)
    )
    unity = jnp.ones_like(vector[..., :1])
    return jnp.concatenate([unity, vector, paired * root_half], -1)


def local_linear(query_feats, key_feats, values, doc_rows, prev_doc):
    tok_rows = values.shape[0]
    head_count = values.shape[1] // DH
    queries = query_feats.astype(jnp.float32).reshape(tok_rows, head_count, F).transpose(1, 0, 2)
    key_rows = key_feats.astype(jnp.float32).reshape(tok_rows, head_count, F).transpose(1, 0, 2)
    value_rows = values.astype(jnp.float32).reshape(tok_rows, head_count, DH).transpose(1, 0, 2)
    scores = jnp.einsum("hif,hjf->hij", queries, key_rows, precision=precise)
    positions = jnp.arange(tok_rows)
    allowed = (positions[None, :] <= positions[:, None]) & (doc_rows[None, :] == doc_rows[:, None])
    weights = jnp.where(allowed[None], 1.0 + scores + 0.5 * scores * scores, 0.0)
    numerator = jnp.einsum("hij,hjd->hid", weights, value_rows, precision=precise)
    denominator = jnp.sum(weights, -1)
    carried = (doc_rows[-1] == prev_doc).astype(jnp.float32)
    select = (doc_rows == doc_rows[-1]).astype(jnp.float32)
    key_phi = taylor(key_rows) * select[None, :, None]
    key_state = jnp.einsum("hje,hjd->hed", key_phi, value_rows, precision=precise)
    key_norm = jnp.sum(key_phi, 1)
    return (numerator, denominator, taylor(queries), key_state, key_norm, carried)


def local(query_feats, key_feats, values, keys_soft, values_soft, norm_gain, doc_ids):
    tok_rows = values.shape[0]
    head_count = values.shape[1] // DH
    kv_heads = keys_soft.shape[1] // DH
    group = head_count // kv_heads
    feature_size = 1 + F + F * F
    seq_count = lax.axis_size("seq")
    seq_index = lax.axis_index("seq")
    is_linear = lax.axis_index("phase") == 0
    first_row = seq_index * tok_rows
    doc_rows = lax.dynamic_slice_in_dim(doc_ids, first_row, tok_rows)
    before_doc = lax.dynamic_index_in_dim(doc_ids, jnp.maximum(first_row - 1, 0), keepdims=False)
    prev_doc = jnp.where(seq_index > 0, before_doc, -1)

    def skip_linear():
        return (
            jnp.zeros((head_count, tok_rows, DH), jnp.float32),
            jnp.zeros((head_count, tok_rows), jnp.float32),
            jnp.zeros((head_count, tok_rows, feature_size), jnp.float32),
            jnp.zeros((head_count, feature_size, DH), jnp.float32),
            jnp.zeros((head_count, feature_size), jnp.float32),
            jnp.zeros((), jnp.float32),
        )

    numerator, denominator, query_phi, key_state, key_norm, carried = lax.cond(
        is_linear,
        lambda: local_linear(query_feats, key_feats, values, doc_rows, prev_doc),
        skip_linear,
    )

    def chain_step(step_index, carried_in):
        total_state, total_norm, got_state, got_norm = carried_in
        got_state, got_norm = from_behind((total_state, total_norm), "seq", 1)
        return (got_state * carried + key_state, got_norm * carried + key_norm, got_state, got_norm)

    initial = (key_state, key_norm, jnp.zeros_like(key_state), jnp.zeros_like(key_norm))
    chained = lax.fori_loop(0, seq_count - 1, chain_step, initial)
    prior_state, prior_norm = (chained[2], chained[3])

    def finish_linear():
        usable = (doc_rows == prev_doc).astype(jnp.float32)
        total_num = numerator + usable[None, :, None] * jnp.einsum(
            "hie,hed->hid", query_phi, prior_state, precision=precise
        )
        total_den = denominator + usable[None, :] * jnp.einsum(
            "hie,he->hi", query_phi, prior_norm, precision=precise
        )
        return (
            (total_num / total_den[..., None])
            .transpose(1, 0, 2)
            .reshape(tok_rows, head_count * DH)
            .astype(jnp.bfloat16)
        )

    linear_out = lax.cond(
        is_linear, finish_linear, lambda: jnp.zeros((tok_rows, head_count * DH), jnp.bfloat16)
    )
    arrived = from_behind(linear_out, "phase", 1)
    widened = arrived.astype(jnp.float32)
    total = lax.psum(jnp.sum(widened * widened, 1), "head")
    all_width = head_count * DH * lax.axis_size("head")
    scale = lax.rsqrt(total / all_width + 1e-06)
    queries = (widened * scale[:, None] * norm_gain[None, :]).astype(jnp.bfloat16)
    query_blocks = queries.reshape(tok_rows, kv_heads, group, DH).transpose(1, 2, 0, 3)
    query_pos = first_row + jnp.arange(tok_rows)

    def attend(carried_in, pieces, first_key):
        key_rows, value_rows = pieces
        span_rows = key_rows.shape[0]
        key_heads = key_rows.reshape(span_rows, kv_heads, DH).transpose(1, 0, 2)
        value_heads = value_rows.reshape(span_rows, kv_heads, DH).transpose(1, 0, 2)
        safe_first = jnp.maximum(first_key, 0)
        key_docs = lax.dynamic_slice_in_dim(doc_ids, safe_first, span_rows)
        key_pos = safe_first + jnp.arange(span_rows)
        allowed = (key_pos[None, :] <= query_pos[:, None]) & (
            key_docs[None, :] == doc_rows[:, None]
        )

        def update():
            running, sums, accum = carried_in
            scores = jnp.einsum(
                "kgcd,kjd->kgcj", query_blocks, key_heads, preferred_element_type=jnp.float32
            ) / math.sqrt(DH)
            scores = jnp.where(allowed, scores, far_below)
            highest = jnp.maximum(running, jnp.max(scores, -1))
            expo = jnp.where(allowed, jnp.exp(scores - highest[..., None]), 0.0)
            rescale = jnp.exp(running - highest)
            mixed_in = jnp.einsum(
                "kgcj,kjd->kgcd",
                expo.astype(jnp.bfloat16),
                value_heads,
                preferred_element_type=jnp.float32,
            )
            return (
                highest,
                sums * rescale + jnp.sum(expo, -1),
                accum * rescale[..., None] + mixed_in,
            )

        active = (
            jnp.logical_not(is_linear) & (first_key >= 0) & (first_key <= first_row + tok_rows - 1)
        )
        return lax.cond(active, update, lambda: carried_in)

    initial = (
        jnp.full((kv_heads, group, tok_rows), far_below, jnp.float32),
        jnp.zeros((kv_heads, group, tok_rows), jnp.float32),
        jnp.zeros((kv_heads, group, tok_rows, DH), jnp.float32),
    )

    def cycle_step(step_index, carried_in):
        pieces, attn_state = carried_in
        source = seq_index - step_index
        attn_state = attend(attn_state, pieces, source * tok_rows)
        pieces = from_behind((pieces[0], pieces[1]), "seq", 1)
        return (pieces, attn_state)

    pieces, attn_state = lax.fori_loop(
        0, seq_count - 1, cycle_step, ((keys_soft, values_soft), initial)
    )
    last_source = seq_index - (seq_count - 1)
    attn_state = attend(attn_state, pieces, last_source * tok_rows)

    def finish_soft():
        result = attn_state[2] / attn_state[1][..., None]
        return result.transpose(2, 0, 1, 3).reshape(tok_rows, head_count * DH).astype(jnp.bfloat16)

    soft_out = lax.cond(
        is_linear, lambda: jnp.zeros((tok_rows, head_count * DH), jnp.bfloat16), finish_soft
    )
    return jnp.where(is_linear, linear_out, soft_out)[None]


def solution(mesh):
    return jax.shard_map(
        local,
        mesh=mesh,
        in_specs=(
            P("seq", "head"),
            P("seq", "head"),
            P("seq", "head"),
            P("seq", "head"),
            P("seq", "head"),
            P("head"),
            P(),
        ),
        out_specs=P("phase", "seq", "head"),
        check_vma=False,
    )
```

profile of v0, /device:TPU:230, one launch (start us, length us, event | category | flops | bytes accessed | tf_op | source)
XLA Modules:
  0.0 726.8 jit_solution(3263422167073176002)
XLA Ops:
  14.4 394.5 %while.40 = (s32[]{:T(128)}, f32[8,273,128]{2,0,1:T(8,128)}, f32[8,273]{1,0:T(8,128)S(1)}, f32[8,273,128]{2,0,1:T(8,128)}, f32[8,273]{1,0:T(8,128)}, /*index=5*/...) while((s32[]{:T(128)}, f32[8,273,128]{2,0,1:T(8,128)}, f32[8,273]{1,0:T(8,128)S(1)}, ...), condition=%wide.region_5.6_spmd, body=%wide.region_4.5_spmd.sunk | while | flops 563474 | bytes 12396621 | solution.py:87
  17.0 26.2 %collective-permute-done.1 = f32[8,273]{1,0:T(8,128)S(1)} collective-permute-done((f32[8,273]{1,0:T(8,128)S(1)}, f32[8,273]{1,0:T(8,128)S(1)}, u32[]{:S(2)}, u32[]{:S(2)}) %collective-permute-start.1) | collective-permute-done | bytes 8768 | tf_op jit(solution)/shard_map/while/body/eval_jaxpr/ppermute | solution.py:20
  47.1 25.3 %collective-permute-done.1 = f32[8,273]{1,0:T(8,128)S(1)} collective-permute-done((f32[8,273]{1,0:T(8,128)S(1)}, f32[8,273]{1,0:T(8,128)S(1)}, u32[]{:S(2)}, u32[]{:S(2)}) %collective-permute-start.1) | collective-permute-done | bytes 8768 | tf_op jit(solution)/shard_map/while/body/eval_jaxpr/ppermute | solution.py:20
  76.4 24.4 %collective-permute-done.1 = f32[8,273]{1,0:T(8,128)S(1)} collective-permute-done((f32[8,273]{1,0:T(8,128)S(1)}, f32[8,273]{1,0:T(8,128)S(1)}, u32[]{:S(2)}, u32[]{:S(2)}) %collective-permute-start.1) | collective-permute-done | bytes 8768 | tf_op jit(solution)/shard_map/while/body/eval_jaxpr/ppermute | solution.py:20
  104.7 23.4 %collective-permute-done.1 = f32[8,273]{1,0:T(8,128)S(1)} collective-permute-done((f32[8,273]{1,0:T(8,128)S(1)}, f32[8,273]{1,0:T(8,128)S(1)}, u32[]{:S(2)}, u32[]{:S(2)}) %collective-permute-start.1) | collective-permute-done | bytes 8768 | tf_op jit(solution)/shard_map/while/body/eval_jaxpr/ppermute | solution.py:20
  132.1 24.3 %collective-permute-done.1 = f32[8,273]{1,0:T(8,128)S(1)} collective-permute-done((f32[8,273]{1,0:T(8,128)S(1)}, f32[8,273]{1,0:T(8,128)S(1)}, u32[]{:S(2)}, u32[]{:S(2)}) %collective-permute-start.1) | collective-permute-done | bytes 8768 | tf_op jit(solution)/shard_map/while/body/eval_jaxpr/ppermute | solution.py:20
  160.3 23.7 %collective-permute-done.1 = f32[8,273]{1,0:T(8,128)S(1)} collective-permute-done((f32[8,273]{1,0:T(8,128)S(1)}, f32[8,273]{1,0:T(8,128)S(1)}, u32[]{:S(2)}, u32[]{:S(2)}) %collective-permute-start.1) | collective-permute-done | bytes 8768 | tf_op jit(solution)/shard_map/while/body/eval_jaxpr/ppermute | solution.py:20
  188.0 22.8 %collective-permute-done.1 = f32[8,273]{1,0:T(8,128)S(1)} collective-permute-done((f32[8,273]{1,0:T(8,128)S(1)}, f32[8,273]{1,0:T(8,128)S(1)}, u32[]{:S(2)}, u32[]{:S(2)}) %collective-permute-start.1) | collective-permute-done | bytes 8768 | tf_op jit(solution)/shard_map/while/body/eval_jaxpr/ppermute | solution.py:20
  214.8 21.9 %collective-permute-done.1 = f32[8,273]{1,0:T(8,128)S(1)} collective-permute-done((f32[8,273]{1,0:T(8,128)S(1)}, f32[8,273]{1,0:T(8,128)S(1)}, u32[]{:S(2)}, u32[]{:S(2)}) %collective-permute-start.1) | collective-permute-done | bytes 8768 | tf_op jit(solution)/shard_map/while/body/eval_jaxpr/ppermute | solution.py:20
  240.6 21.1 %collective-permute-done.1 = f32[8,273]{1,0:T(8,128)S(1)} collective-permute-done((f32[8,273]{1,0:T(8,128)S(1)}, f32[8,273]{1,0:T(8,128)S(1)}, u32[]{:S(2)}, u32[]{:S(2)}) %collective-permute-start.1) | collective-permute-done | bytes 8768 | tf_op jit(solution)/shard_map/while/body/eval_jaxpr/ppermute | solution.py:20
  265.7 21.1 %collective-permute-done.1 = f32[8,273]{1,0:T(8,128)S(1)} collective-permute-done((f32[8,273]{1,0:T(8,128)S(1)}, f32[8,273]{1,0:T(8,128)S(1)}, u32[]{:S(2)}, u32[]{:S(2)}) %collective-permute-start.1) | collective-permute-done | bytes 8768 | tf_op jit(solution)/shard_map/while/body/eval_jaxpr/ppermute | solution.py:20
  290.7 21.1 %collective-permute-done.1 = f32[8,273]{1,0:T(8,128)S(1)} collective-permute-done((f32[8,273]{1,0:T(8,128)S(1)}, f32[8,273]{1,0:T(8,128)S(1)}, u32[]{:S(2)}, u32[]{:S(2)}) %collective-permute-start.1) | collective-permute-done | bytes 8768 | tf_op jit(solution)/shard_map/while/body/eval_jaxpr/ppermute | solution.py:20
  315.8 21.1 %collective-permute-done.1 = f32[8,273]{1,0:T(8,128)S(1)} collective-permute-done((f32[8,273]{1,0:T(8,128)S(1)}, f32[8,273]{1,0:T(8,128)S(1)}, u32[]{:S(2)}, u32[]{:S(2)}) %collective-permute-start.1) | collective-permute-done | bytes 8768 | tf_op jit(solution)/shard_map/while/body/eval_jaxpr/ppermute | solution.py:20
  340.9 21.1 %collective-permute-done.1 = f32[8,273]{1,0:T(8,128)S(1)} collective-permute-done((f32[8,273]{1,0:T(8,128)S(1)}, f32[8,273]{1,0:T(8,128)S(1)}, u32[]{:S(2)}, u32[]{:S(2)}) %collective-permute-start.1) | collective-permute-done | bytes 8768 | tf_op jit(solution)/shard_map/while/body/eval_jaxpr/ppermute | solution.py:20
  366.0 21.3 %collective-permute-done.1 = f32[8,273]{1,0:T(8,128)S(1)} collective-permute-done((f32[8,273]{1,0:T(8,128)S(1)}, f32[8,273]{1,0:T(8,128)S(1)}, u32[]{:S(2)}, u32[]{:S(2)}) %collective-permute-start.1) | collective-permute-done | bytes 8768 | tf_op jit(solution)/shard_map/while/body/eval_jaxpr/ppermute | solution.py:20
  391.2 16.3 %collective-permute-done.1 = f32[8,273]{1,0:T(8,128)S(1)} collective-permute-done((f32[8,273]{1,0:T(8,128)S(1)}, f32[8,273]{1,0:T(8,128)S(1)}, u32[]{:S(2)}, u32[]{:S(2)}) %collective-permute-start.1) | collective-permute-done | bytes 8768 | tf_op jit(solution)/shard_map/while/body/eval_jaxpr/ppermute | solution.py:20
  414.6 40.8 %collective-permute-done.4 = bf16[512,1024]{0,1:T(8,128)(2,1)S(1)} collective-permute-done((bf16[512,1024]{0,1:T(8,128)(2,1)}, bf16[512,1024]{0,1:T(8,128)(2,1)S(1)}, u32[]{:S(2)}, u32[]{:S(2)}) %collective-permute-start.4) | collective-permute-done | bytes 1048608 | tf_op jit(solution)/shard_map/ppermute | solution.py:20
  455.6 12.6 %psum.7 = f32[512]{0:T(512)S(1)} all-reduce(f32[512]{0:T(512)S(1)} %fusion.60), channel_id=1, replica_groups=mesh['phase'=2,'seq'=16,'head'=8] {'head'}, use_global_device_ids=true, to_apply=%region_9.10 | all-reduce | flops 512 | bytes 4096 | tf_op jit(solution)/shard_map/psum | solution.py:110
  470.7 243.8 %while.41 = (s32[]{:T(128)}, bf16[512,128]{1,0:T(8,128)(2,1)S(1)}, bf16[512,128]{1,0:T(8,128)(2,1)S(1)}, f32[1,8,512]{2,1,0:T(8,128)S(1)}, f32[1,8,512]{2,1,0:T(...) while((s32[]{:T(128)}, bf16[512,128]{1,0:T(8,128)(2,1)S(1)}, ...), condition=%wide.region_15.16_spmd.clone, body=%wide.region_10.15_spmd.clone.sunk | while | flops 1102853120 | bytes 50356736 | solution.py:168
  504.5 11.0 %conditional.11 = ((f32[1,8,512]{2,1,0:T(8,128)S(1)}, f32[1,8,512]{2,1,0:T(8,128)S(1)}, f32[1,8,512,128]{3,2,1,0:T(8,128)})) conditional(s32[]{:T(128)} %convert_element_type.90, (f32[1,8,512]{2,1,0:T(8,128)S(1)}, f32[1,8,512]{2,1,0:T(8,128)S(1)}, f32[1,8,512,128]{3,2,1,0:T(8,128)}) %tuple.116, (s32[]{:T(128)}, s32[1,512]{1,0:T(1,128)S(1)}, ...), branch_computations={%region_11.11_spmd, %region_12.14_spmd} | conditional | flops 1102853120 | bytes 48779376 | solution.py:153
  556.4 11.0 %conditional.11 = ((f32[1,8,512]{2,1,0:T(8,128)S(1)}, f32[1,8,512]{2,1,0:T(8,128)S(1)}, f32[1,8,512,128]{3,2,1,0:T(8,128)})) conditional(s32[]{:T(128)} %convert_element_type.90, (f32[1,8,512]{2,1,0:T(8,128)S(1)}, f32[1,8,512]{2,1,0:T(8,128)S(1)}, f32[1,8,512,128]{3,2,1,0:T(8,128)}) %tuple.116, (s32[]{:T(128)}, s32[1,512]{1,0:T(1,128)S(1)}, ...), branch_computations={%region_11.11_spmd, %region_12.14_spmd} | conditional | flops 1102853120 | bytes 48779376 | solution.py:153
  588.8 11.0 %conditional.11 = ((f32[1,8,512]{2,1,0:T(8,128)S(1)}, f32[1,8,512]{2,1,0:T(8,128)S(1)}, f32[1,8,512,128]{3,2,1,0:T(8,128)})) conditional(s32[]{:T(128)} %convert_element_type.90, (f32[1,8,512]{2,1,0:T(8,128)S(1)}, f32[1,8,512]{2,1,0:T(8,128)S(1)}, f32[1,8,512,128]{3,2,1,0:T(8,128)}) %tuple.116, (s32[]{:T(128)}, s32[1,512]{1,0:T(1,128)S(1)}, ...), branch_computations={%region_11.11_spmd, %region_12.14_spmd} | conditional | flops 1102853120 | bytes 48779376 | solution.py:153
  637.4 11.0 %conditional.11 = ((f32[1,8,512]{2,1,0:T(8,128)S(1)}, f32[1,8,512]{2,1,0:T(8,128)S(1)}, f32[1,8,512,128]{3,2,1,0:T(8,128)})) conditional(s32[]{:T(128)} %convert_element_type.90, (f32[1,8,512]{2,1,0:T(8,128)S(1)}, f32[1,8,512]{2,1,0:T(8,128)S(1)}, f32[1,8,512,128]{3,2,1,0:T(8,128)}) %tuple.116, (s32[]{:T(128)}, s32[1,512]{1,0:T(1,128)S(1)}, ...), branch_computations={%region_11.11_spmd, %region_12.14_spmd} | conditional | flops 1102853120 | bytes 48779376 | solution.py:153
  686.1 11.0 %conditional.11 = ((f32[1,8,512]{2,1,0:T(8,128)S(1)}, f32[1,8,512]{2,1,0:T(8,128)S(1)}, f32[1,8,512,128]{3,2,1,0:T(8,128)})) conditional(s32[]{:T(128)} %convert_element_type.90, (f32[1,8,512]{2,1,0:T(8,128)S(1)}, f32[1,8,512]{2,1,0:T(8,128)S(1)}, f32[1,8,512,128]{3,2,1,0:T(8,128)}) %tuple.116, (s32[]{:T(128)}, s32[1,512]{1,0:T(1,128)S(1)}, ...), branch_computations={%region_11.11_spmd, %region_12.14_spmd} | conditional | flops 1102853120 | bytes 48779376 | solution.py:153
  (527 shorter events, 459.1 us)
Async XLA Ops:
  14.4 28.8 %collective-permute-start = (f32[8,273,128]{2,0,1:T(8,128)}, f32[8,273,128]{2,0,1:T(8,128)S(1)}, u32[]{:S(2)}, u32[]{:S(2)}) collective-permute-start(f32[8,273,128]{2,0,1:T(8,128)} %get-tuple-element.854), channel_id=1, source_target_pairs={{0,8},{8,16},{16,24},{24,32},{32,40},{40,48},{48,56},{56,64},{64,7... | collective-permute-start | bytes 3354632 | tf_op jit(solution)/shard_map/while/body/eval_jaxpr/ppermute | solution.py:20
  15.7 27.5 %collective-permute-start.1 = (f32[8,273]{1,0:T(8,128)S(1)}, f32[8,273]{1,0:T(8,128)S(1)}, u32[]{:S(2)}, u32[]{:S(2)}) collective-permute-start(f32[8,273]{1,0:T(8,128)S(1)} %get-tuple-element.855), channel_id=1, source_target_pairs={{0,8},{8,16},{16,24},{24,32},{32,40},{40,48},{48,56},{56,64},{64,7... | collective-permute-start | bytes 26216 | tf_op jit(solution)/shard_map/while/body/eval_jaxpr/ppermute | solution.py:20
  44.6 27.9 %collective-permute-start = (f32[8,273,128]{2,0,1:T(8,128)}, f32[8,273,128]{2,0,1:T(8,128)S(1)}, u32[]{:S(2)}, u32[]{:S(2)}) collective-permute-start(f32[8,273,128]{2,0,1:T(8,128)} %get-tuple-element.854), channel_id=1, source_target_pairs={{0,8},{8,16},{16,24},{24,32},{32,40},{40,48},{48,56},{56,64},{64,7... | collective-permute-start | bytes 3354632 | tf_op jit(solution)/shard_map/while/body/eval_jaxpr/ppermute | solution.py:20
  45.8 26.6 %collective-permute-start.1 = (f32[8,273]{1,0:T(8,128)S(1)}, f32[8,273]{1,0:T(8,128)S(1)}, u32[]{:S(2)}, u32[]{:S(2)}) collective-permute-start(f32[8,273]{1,0:T(8,128)S(1)} %get-tuple-element.855), channel_id=1, source_target_pairs={{0,8},{8,16},{16,24},{24,32},{32,40},{40,48},{48,56},{56,64},{64,7... | collective-permute-start | bytes 26216 | tf_op jit(solution)/shard_map/while/body/eval_jaxpr/ppermute | solution.py:20
  73.8 27.0 %collective-permute-start = (f32[8,273,128]{2,0,1:T(8,128)}, f32[8,273,128]{2,0,1:T(8,128)S(1)}, u32[]{:S(2)}, u32[]{:S(2)}) collective-permute-start(f32[8,273,128]{2,0,1:T(8,128)} %get-tuple-element.854), channel_id=1, source_target_pairs={{0,8},{8,16},{16,24},{24,32},{32,40},{40,48},{48,56},{56,64},{64,7... | collective-permute-start | bytes 3354632 | tf_op jit(solution)/shard_map/while/body/eval_jaxpr/ppermute | solution.py:20
  75.1 25.7 %collective-permute-start.1 = (f32[8,273]{1,0:T(8,128)S(1)}, f32[8,273]{1,0:T(8,128)S(1)}, u32[]{:S(2)}, u32[]{:S(2)}) collective-permute-start(f32[8,273]{1,0:T(8,128)S(1)} %get-tuple-element.855), channel_id=1, source_target_pairs={{0,8},{8,16},{16,24},{24,32},{32,40},{40,48},{48,56},{56,64},{64,7... | collective-permute-start | bytes 26216 | tf_op jit(solution)/shard_map/while/body/eval_jaxpr/ppermute | solution.py:20
  102.1 26.0 %collective-permute-start = (f32[8,273,128]{2,0,1:T(8,128)}, f32[8,273,128]{2,0,1:T(8,128)S(1)}, u32[]{:S(2)}, u32[]{:S(2)}) collective-permute-start(f32[8,273,128]{2,0,1:T(8,128)} %get-tuple-element.854), channel_id=1, source_target_pairs={{0,8},{8,16},{16,24},{24,32},{32,40},{40,48},{48,56},{56,64},{64,7... | collective-permute-start | bytes 3354632 | tf_op jit(solution)/shard_map/while/body/eval_jaxpr/ppermute | solution.py:20
  103.4 24.7 %collective-permute-start.1 = (f32[8,273]{1,0:T(8,128)S(1)}, f32[8,273]{1,0:T(8,128)S(1)}, u32[]{:S(2)}, u32[]{:S(2)}) collective-permute-start(f32[8,273]{1,0:T(8,128)S(1)} %get-tuple-element.855), channel_id=1, source_target_pairs={{0,8},{8,16},{16,24},{24,32},{32,40},{40,48},{48,56},{56,64},{64,7... | collective-permute-start | bytes 26216 | tf_op jit(solution)/shard_map/while/body/eval_jaxpr/ppermute | solution.py:20
  129.5 26.9 %collective-permute-start = (f32[8,273,128]{2,0,1:T(8,128)}, f32[8,273,128]{2,0,1:T(8,128)S(1)}, u32[]{:S(2)}, u32[]{:S(2)}) collective-permute-start(f32[8,273,128]{2,0,1:T(8,128)} %get-tuple-element.854), channel_id=1, source_target_pairs={{0,8},{8,16},{16,24},{24,32},{32,40},{40,48},{48,56},{56,64},{64,7... | collective-permute-start | bytes 3354632 | tf_op jit(solution)/shard_map/while/body/eval_jaxpr/ppermute | solution.py:20
  130.8 25.6 %collective-permute-start.1 = (f32[8,273]{1,0:T(8,128)S(1)}, f32[8,273]{1,0:T(8,128)S(1)}, u32[]{:S(2)}, u32[]{:S(2)}) collective-permute-start(f32[8,273]{1,0:T(8,128)S(1)} %get-tuple-element.855), channel_id=1, source_target_pairs={{0,8},{8,16},{16,24},{24,32},{32,40},{40,48},{48,56},{56,64},{64,7... | collective-permute-start | bytes 26216 | tf_op jit(solution)/shard_map/while/body/eval_jaxpr/ppermute | solution.py:20
  157.8 26.3 %collective-permute-start = (f32[8,273,128]{2,0,1:T(8,128)}, f32[8,273,128]{2,0,1:T(8,128)S(1)}, u32[]{:S(2)}, u32[]{:S(2)}) collective-permute-start(f32[8,273,128]{2,0,1:T(8,128)} %get-tuple-element.854), channel_id=1, source_target_pairs={{0,8},{8,16},{16,24},{24,32},{32,40},{40,48},{48,56},{56,64},{64,7... | collective-permute-start | bytes 3354632 | tf_op jit(solution)/shard_map/while/body/eval_jaxpr/ppermute | solution.py:20
  159.0 25.0 %collective-permute-start.1 = (f32[8,273]{1,0:T(8,128)S(1)}, f32[8,273]{1,0:T(8,128)S(1)}, u32[]{:S(2)}, u32[]{:S(2)}) collective-permute-start(f32[8,273]{1,0:T(8,128)S(1)} %get-tuple-element.855), channel_id=1, source_target_pairs={{0,8},{8,16},{16,24},{24,32},{32,40},{40,48},{48,56},{56,64},{64,7... | collective-permute-start | bytes 26216 | tf_op jit(solution)/shard_map/while/body/eval_jaxpr/ppermute | solution.py:20
  185.4 25.4 %collective-permute-start = (f32[8,273,128]{2,0,1:T(8,128)}, f32[8,273,128]{2,0,1:T(8,128)S(1)}, u32[]{:S(2)}, u32[]{:S(2)}) collective-permute-start(f32[8,273,128]{2,0,1:T(8,128)} %get-tuple-element.854), channel_id=1, source_target_pairs={{0,8},{8,16},{16,24},{24,32},{32,40},{40,48},{48,56},{56,64},{64,7... | collective-permute-start | bytes 3354632 | tf_op jit(solution)/shard_map/while/body/eval_jaxpr/ppermute | solution.py:20
  186.7 24.1 %collective-permute-start.1 = (f32[8,273]{1,0:T(8,128)S(1)}, f32[8,273]{1,0:T(8,128)S(1)}, u32[]{:S(2)}, u32[]{:S(2)}) collective-permute-start(f32[8,273]{1,0:T(8,128)S(1)} %get-tuple-element.855), channel_id=1, source_target_pairs={{0,8},{8,16},{16,24},{24,32},{32,40},{40,48},{48,56},{56,64},{64,7... | collective-permute-start | bytes 26216 | tf_op jit(solution)/shard_map/while/body/eval_jaxpr/ppermute | solution.py:20
  212.2 24.5 %collective-permute-start = (f32[8,273,128]{2,0,1:T(8,128)}, f32[8,273,128]{2,0,1:T(8,128)S(1)}, u32[]{:S(2)}, u32[]{:S(2)}) collective-permute-start(f32[8,273,128]{2,0,1:T(8,128)} %get-tuple-element.854), channel_id=1, source_target_pairs={{0,8},{8,16},{16,24},{24,32},{32,40},{40,48},{48,56},{56,64},{64,7... | collective-permute-start | bytes 3354632 | tf_op jit(solution)/shard_map/while/body/eval_jaxpr/ppermute | solution.py:20
  213.5 23.2 %collective-permute-start.1 = (f32[8,273]{1,0:T(8,128)S(1)}, f32[8,273]{1,0:T(8,128)S(1)}, u32[]{:S(2)}, u32[]{:S(2)}) collective-permute-start(f32[8,273]{1,0:T(8,128)S(1)} %get-tuple-element.855), channel_id=1, source_target_pairs={{0,8},{8,16},{16,24},{24,32},{32,40},{40,48},{48,56},{56,64},{64,7... | collective-permute-start | bytes 26216 | tf_op jit(solution)/shard_map/while/body/eval_jaxpr/ppermute | solution.py:20
  238.0 23.7 %collective-permute-start = (f32[8,273,128]{2,0,1:T(8,128)}, f32[8,273,128]{2,0,1:T(8,128)S(1)}, u32[]{:S(2)}, u32[]{:S(2)}) collective-permute-start(f32[8,273,128]{2,0,1:T(8,128)} %get-tuple-element.854), channel_id=1, source_target_pairs={{0,8},{8,16},{16,24},{24,32},{32,40},{40,48},{48,56},{56,64},{64,7... | collective-permute-start | bytes 3354632 | tf_op jit(solution)/shard_map/while/body/eval_jaxpr/ppermute | solution.py:20
  263.1 23.7 %collective-permute-start = (f32[8,273,128]{2,0,1:T(8,128)}, f32[8,273,128]{2,0,1:T(8,128)S(1)}, u32[]{:S(2)}, u32[]{:S(2)}) collective-permute-start(f32[8,273,128]{2,0,1:T(8,128)} %get-tuple-element.854), channel_id=1, source_target_pairs={{0,8},{8,16},{16,24},{24,32},{32,40},{40,48},{48,56},{56,64},{64,7... | collective-permute-start | bytes 3354632 | tf_op jit(solution)/shard_map/while/body/eval_jaxpr/ppermute | solution.py:20
  288.2 23.7 %collective-permute-start = (f32[8,273,128]{2,0,1:T(8,128)}, f32[8,273,128]{2,0,1:T(8,128)S(1)}, u32[]{:S(2)}, u32[]{:S(2)}) collective-permute-start(f32[8,273,128]{2,0,1:T(8,128)} %get-tuple-element.854), channel_id=1, source_target_pairs={{0,8},{8,16},{16,24},{24,32},{32,40},{40,48},{48,56},{56,64},{64,7... | collective-permute-start | bytes 3354632 | tf_op jit(solution)/shard_map/while/body/eval_jaxpr/ppermute | solution.py:20
  313.2 23.7 %collective-permute-start = (f32[8,273,128]{2,0,1:T(8,128)}, f32[8,273,128]{2,0,1:T(8,128)S(1)}, u32[]{:S(2)}, u32[]{:S(2)}) collective-permute-start(f32[8,273,128]{2,0,1:T(8,128)} %get-tuple-element.854), channel_id=1, source_target_pairs={{0,8},{8,16},{16,24},{24,32},{32,40},{40,48},{48,56},{56,64},{64,7... | collective-permute-start | bytes 3354632 | tf_op jit(solution)/shard_map/while/body/eval_jaxpr/ppermute | solution.py:20
  338.3 23.7 %collective-permute-start = (f32[8,273,128]{2,0,1:T(8,128)}, f32[8,273,128]{2,0,1:T(8,128)S(1)}, u32[]{:S(2)}, u32[]{:S(2)}) collective-permute-start(f32[8,273,128]{2,0,1:T(8,128)} %get-tuple-element.854), channel_id=1, source_target_pairs={{0,8},{8,16},{16,24},{24,32},{32,40},{40,48},{48,56},{56,64},{64,7... | collective-permute-start | bytes 3354632 | tf_op jit(solution)/shard_map/while/body/eval_jaxpr/ppermute | solution.py:20
  363.4 23.9 %collective-permute-start = (f32[8,273,128]{2,0,1:T(8,128)}, f32[8,273,128]{2,0,1:T(8,128)S(1)}, u32[]{:S(2)}, u32[]{:S(2)}) collective-permute-start(f32[8,273,128]{2,0,1:T(8,128)} %get-tuple-element.854), channel_id=1, source_target_pairs={{0,8},{8,16},{16,24},{24,32},{32,40},{40,48},{48,56},{56,64},{64,7... | collective-permute-start | bytes 3354632 | tf_op jit(solution)/shard_map/while/body/eval_jaxpr/ppermute | solution.py:20
  364.7 22.6 %collective-permute-start.1 = (f32[8,273]{1,0:T(8,128)S(1)}, f32[8,273]{1,0:T(8,128)S(1)}, u32[]{:S(2)}, u32[]{:S(2)}) collective-permute-start(f32[8,273]{1,0:T(8,128)S(1)} %get-tuple-element.855), channel_id=1, source_target_pairs={{0,8},{8,16},{16,24},{24,32},{32,40},{40,48},{48,56},{56,64},{64,7... | collective-permute-start | bytes 26216 | tf_op jit(solution)/shard_map/while/body/eval_jaxpr/ppermute | solution.py:20
  409.9 45.4 %collective-permute-start.4 = (bf16[512,1024]{0,1:T(8,128)(2,1)}, bf16[512,1024]{0,1:T(8,128)(2,1)S(1)}, u32[]{:S(2)}, u32[]{:S(2)}) collective-permute-start(bf16[512,1024]{0,1:T(8,128)(2,1)} %get-tuple-element.923), channel_id=1, source_target_pairs={{0,128},{1,129},{2,130},{3,131},{4,132},{5,133},{6,134},{7,135},{8... | collective-permute-start | bytes 3145736 | tf_op jit(solution)/shard_map/ppermute | solution.py:20
  (105 other events, 851.0 us)
where the time goes:
time: 741 us; the launch traced here: 727 us
  waiting for transfers between devices  396 us (53%)
  matrix products  102 us (14%)
  starting transfers between devices  78.3 us (11%)
  local copies, waits for them, and re-layouts  66.9 us (9%)
  other arithmetic  60.2 us (8%)
  blocking collectives  12.6 us (2%)
  loops' own time  10 us (1%)
    ppermute x61, waiting for transfers between devices, from_behind(): return lax.ppermute(x, axis, pairs)  396 us
    ppermute x61, starting transfers between devices, from_behind(): return lax.ppermute(x, axis, pairs)  78.3 us
    dot_general x16, matrix products, update(): jnp.einsum('kgcj,kjd->kgcd', expo.astype(jnp.bfloat16), value_heads, pref...  63.5 us
    dot_general x16, matrix products, update(): jnp.einsum('kgcd,kjd->kgcj', query_blocks, key_heads, preferred_element_t...  38.6 us
    reduce_sum x16, other arithmetic, update(): jnp.sum(expo, -1)  32.5 us
    while x90, local copies, waits for them, and re-layouts  21.8 us
    cond x82, local copies, waits for them, and re-layouts  20.4 us
    add x15, other arithmetic, chain_step(): got_state * carried + key_state  18.3 us
  transfers between devices with their start and end apart: 61, of which 30 were waited for; matrix products, arithmetic and copies ran while one was open for 22% of the time, Pallas kernels for 0%

commit v1 on v0

v1 whole, which is shorter than its diff:
```python
import math

import jax
import jax.numpy as jnp
from jax import lax
from jax.experimental import pallas as pl
from jax.experimental.pallas import tpu as pltpu
from jax.sharding import Mesh, PartitionSpec as P

DH = 128
F = 16
ROWS = 512
HEADS = 8
WIDE = HEADS * DH
ALL_WIDE = 64 * DH
USED = (F + 1) * (F + 2) // 2
FEATS = 160
QUARTER = HEADS * FEATS // 4
SLOTS = 9
LOG2E = math.log2(math.e)
FACTOR = LOG2E / math.sqrt(DH)
SAFE = 110.0
FAR = -1e30

NN = (((1,), (0,)), ((), ()))
NT = (((1,), (1,)), ((), ()))


def dot(a, b, dims=NN):
    return lax.dot_general(a, b, dims, preferred_element_type=jnp.float32)


def split(x):
    hi = x.astype(jnp.bfloat16)
    lo = (x - hi.astype(jnp.float32)).astype(jnp.bfloat16)
    return hi, lo


def doc_of(position, n1, n2):
    return (position >= n1).astype(jnp.int32) + (position >= n2).astype(jnp.int32)


def start_of(position, n1, n2):
    return jnp.where(position >= n2, n2, jnp.where(position >= n1, n1, 0))


def pair_of(e):
    gap = jnp.zeros_like(e)
    for k in range(1, F // 2 + 1):
        gap = gap + (e >= k * (F + 1)).astype(jnp.int32)
    m = e - gap * (F + 1)
    n = m + gap
    n = jnp.where(n > F, n - (F + 1), n)
    times = jnp.where((gap == 0) & (m < F), 1.0, 2.0)
    times = jnp.where(e < USED, times, 0.0)
    return m, n, times


def here():
    return lax.axis_index("z"), lax.axis_index("x")


def row_block(x, s):
    return lax.rem(x - s + 4, 4)


def last_doc(block, n1, n2):
    return doc_of(block * ROWS + ROWS - 1, n1, n2)


def flag(x):
    return x.astype(jnp.float32)


def row_sum_kernel(n_ref, p0_ref, p1_ref, p2_ref, p3_ref, out_ref):
    n1, n2 = n_ref[0], n_ref[1]
    z, x = here()
    end = last_doc(z * 4 + 3, n1, n2)
    total = jnp.zeros((QUARTER, DH), jnp.float32)
    for s, part in enumerate((p0_ref, p1_ref, p2_ref, p3_ref)):
        total = total + flag(last_doc(z * 4 + row_block(x, s), n1, n2) == end) * part[...]
    out_ref[...] = total


def prior_kernel(n_ref, p0_ref, p1_ref, p2_ref, p3_ref, near_ref, far_ref, *outs):
    n1, n2 = n_ref[0], n_ref[1]
    z, x = here()
    before = last_doc(z * 4 - 1, n1, n2)
    incoming = near_ref[...] + flag(last_doc(z * 4 - 5, n1, n2) == before) * far_ref[...]
    for t, out in enumerate(outs):
        target = lax.rem(x + t, 4)
        doc = last_doc(z * 4 + target - 1, n1, n2)
        prior = flag(before == doc) * incoming
        for s, part in enumerate((p0_ref, p1_ref, p2_ref, p3_ref)):
            block = row_block(x, s)
            prior = prior + flag((block < target) & (last_doc(z * 4 + block, n1, n2) == doc)) * part[...]
        out[...] = prior


def pack_kernel(own_hbm, near_hbm, far_hbm, o1_hbm, o2_hbm, o3_hbm, sems):
    z, x = here()
    upper, lower = pl.ds(0, 2 * ROWS), pl.ds(2 * ROWS, 2 * ROWS)
    for s, out in enumerate((o1_hbm, o2_hbm, o3_hbm)):
        later = lax.rem(x + s + 1, 4) > x
        pltpu.make_async_copy(near_hbm, out.at[upper], sems.at[s]).start()
        pl.when(later)(lambda: pltpu.make_async_copy(own_hbm, out.at[lower], sems.at[3 + s]).start())
        pl.when(jnp.logical_not(later))(lambda: pltpu.make_async_copy(far_hbm, out.at[lower], sems.at[3 + s]).start())
    for s, out in enumerate((o1_hbm, o2_hbm, o3_hbm)):
        pltpu.make_async_copy(near_hbm, out.at[upper], sems.at[s]).wait()
        pltpu.make_async_copy(own_hbm, out.at[lower], sems.at[3 + s]).wait()


def states_kernel(doc_hbm, kf_hbm, v_hbm, k_hbm, vs_hbm, c0_ref, c1_ref, c2_ref, c3_ref, kv_ref, n_ref, state_ref, doc_ref, kf_ref, v_ref, sems):
    pairs = [(doc_hbm, doc_ref), (kf_hbm, kf_ref), (v_hbm, v_ref), (k_hbm, kv_ref.at[:ROWS]), (vs_hbm, kv_ref.at[ROWS:])]
    copies = [pltpu.make_async_copy(src, dst, sems.at[i]) for i, (src, dst) in enumerate(pairs)]
    for copy in copies:
        copy.start()
    z, x = here()
    first = (z * 4 + x) * ROWS
    m, n, times = pair_of(lax.broadcasted_iota(jnp.int32, (FEATS, 2 * F), 0))
    col = lax.broadcasted_iota(jnp.int32, (FEATS, 2 * F), 1)
    e1 = ((col == m) & (times > 0)).astype(jnp.float32).astype(jnp.bfloat16)
    e2 = ((col == n) & (times > 0)).astype(jnp.float32).astype(jnp.bfloat16)
    lane = lax.broadcasted_iota(jnp.int32, (ROWS, DH), 1)
    norms = jnp.zeros((FEATS, DH), jnp.float32)
    copies[0].wait()
    n1 = jnp.sum((doc_ref[...] < 1).astype(jnp.int32))
    n2 = jnp.sum((doc_ref[...] < 2).astype(jnp.int32))
    n_ref[0] = n1
    n_ref[1] = n2
    pos = first + lax.broadcasted_iota(jnp.int32, (F, ROWS), 1)
    sel = (doc_of(pos, n1, n2) == doc_of(first + ROWS - 1, n1, n2)).astype(jnp.float32)
    copies[1].wait()
    kt = kf_ref[...].astype(jnp.float32).T
    copies[2].wait()
    for h in range(HEADS):
        rows = jnp.concatenate([kt[h * F : (h + 1) * F] * sel, sel], 0).astype(jnp.bfloat16)
        hi, lo = split(dot(e1, rows) * dot(e2, rows))
        unit = (lane == h).astype(jnp.bfloat16)
        rhs = jnp.concatenate([v_ref[:, h * DH : (h + 1) * DH], unit], 1)
        res = dot(hi, rhs) + dot(lo, rhs)
        state_ref[h * FEATS : (h + 1) * FEATS, :] = res[:, :DH]
        norms = norms + res[:, DH:]
    across = norms.T
    for h in range(HEADS):
        base = h * FEATS + USED
        state_ref[base : base + 1, :] = across[h : h + 1, :DH]
        state_ref[base + 1 : base + 2, : FEATS - DH] = across[h : h + 1, DH:]
    for s, out in enumerate((c0_ref, c1_ref, c2_ref, c3_ref)):
        chunk = lax.rem(x + s, 4)
        out[...] = state_ref[pl.ds(pl.multiple_of(chunk * QUARTER, QUARTER), QUARTER), :]
    copies[3].wait()
    copies[4].wait()


def local_kernel(n_ref, qf_ref, kf_ref, v_ref, num_ref, den_ref, hi_ref, lo_ref, mask_ref):
    n1, n2 = n_ref[0], n_ref[1]
    z, x = here()
    first = (z * 4 + x) * ROWS
    row = lax.broadcasted_iota(jnp.int32, (ROWS, ROWS), 0)
    col = lax.broadcasted_iota(jnp.int32, (ROWS, ROWS), 1)
    begin = start_of(first + lax.broadcasted_iota(jnp.int32, (ROWS, 1), 0), n1, n2) - first
    mask_ref[...] = ((col <= row) & (col >= begin)).astype(jnp.float32)
    lane = lax.broadcasted_iota(jnp.int32, (ROWS, DH), 1)
    one = (lane == 0).astype(jnp.bfloat16)
    kf = jnp.concatenate([kf_ref[...], one], 1)
    half = ROWS // 2
    dens = [jnp.zeros((half, DH), jnp.float32) for _ in range(2)]
    for h in range(HEADS):
        qh = jnp.where(lane // F == h, qf_ref[...], jnp.zeros((), jnp.bfloat16))
        qh = jnp.concatenate([qh, one], 1)
        unit = (lane == h).astype(jnp.bfloat16)
        rhs = jnp.concatenate([v_ref[:, h * DH : (h + 1) * DH], unit], 1)
        for r in range(2):
            span = (r + 1) * half
            s = dot(qh[r * half : (r + 1) * half], kf[:span], NT)
            w = (s * s + 1.0) * mask_ref[r * half : (r + 1) * half, :span]
            hi, lo = split(w)
            res = dot(hi, rhs[:span]) + dot(lo, rhs[:span])
            num_ref[r * half : (r + 1) * half, h * DH : (h + 1) * DH] = res[:, :DH]
            dens[r] = dens[r] + res[:, DH:]
    for r in range(2):
        den_ref[r * half : (r + 1) * half, :] = dens[r]
    m, n, times = pair_of(lax.broadcasted_iota(jnp.int32, (DH, 256), 1))
    lane_row = lax.broadcasted_iota(jnp.int32, (DH, 256), 0)
    m1, n1_, times1 = pair_of(lax.broadcasted_iota(jnp.int32, (1, 256), 1))
    ones_a = jnp.where(m1 == F, times1, 0.0)
    ones_b = jnp.where((n1_ == F) & (times1 > 0), 1.0, 0.0)
    once = (times > 0).astype(jnp.float32)
    q = qf_ref[...]
    for h in range(HEADS):
        e1 = jnp.where((lane_row == m + h * F) & (m < F), times, 0.0).astype(jnp.bfloat16)
        e2 = jnp.where((lane_row == n + h * F) & (n < F), once, 0.0).astype(jnp.bfloat16)
        hi, lo = split((dot(q, e1) + ones_a) * (dot(q, e2) + ones_b))
        hi_ref[:, h * 256 : (h + 1) * 256] = hi
        lo_ref[:, h * 256 : (h + 1) * 256] = lo


def finish_kernel(n_ref, hi_ref, lo_ref, num_ref, den_ref, p0_ref, p1_ref, p2_ref, p3_ref, out_ref, sq_ref, prior_ref):
    n1, n2 = n_ref[0], n_ref[1]
    z, x = here()
    first = (z * 4 + x) * ROWS
    pos = first + lax.broadcasted_iota(jnp.int32, (ROWS, 1), 0)
    usable = ((doc_of(pos, n1, n2) == doc_of(first - 1, n1, n2)) & (first > 0)).astype(jnp.float32)
    for s, part in enumerate((p0_ref, p1_ref, p2_ref, p3_ref)):
        chunk = lax.rem(x - s + 4, 4)
        prior_ref[pl.ds(pl.multiple_of(chunk * QUARTER, QUARTER), QUARTER), :] = part[...]
    spare = [jnp.zeros((DH - HEADS, DH), jnp.float32)]
    sums = [[prior_ref[h * FEATS + USED + i : h * FEATS + USED + i + 1, :] for h in range(HEADS)] for i in range(2)]
    norm = jnp.concatenate([jnp.concatenate(rows + spare, 0).T for rows in sums], 0)[:FEATS]
    norm_hi, norm_lo = split(norm)
    squares = jnp.zeros((ROWS, DH), jnp.float32)
    for h in range(HEADS):
        hi = hi_ref[:, h * 256 : h * 256 + FEATS]
        lo = lo_ref[:, h * 256 : h * 256 + FEATS]
        s_hi, s_lo = split(prior_ref[h * FEATS : (h + 1) * FEATS, :])
        r_hi = jnp.concatenate([s_hi, norm_hi], 1)
        r_lo = jnp.concatenate([s_lo, norm_lo], 1)
        res = (dot(hi, r_hi) + (dot(lo, r_hi) + dot(hi, r_lo))) * usable
        num = num_ref[:, h * DH : (h + 1) * DH] + res[:, :DH]
        den = den_ref[:, h : h + 1] + res[:, DH + h : DH + h + 1]
        out = (num / den).astype(jnp.bfloat16)
        out_ref[:, h * DH : (h + 1) * DH] = out
        wide = out.astype(jnp.float32)
        squares = squares + wide * wide
    sq_ref[...] = jnp.sum(squares.T, 0, keepdims=True)


def block_of(slot):
    z, x = here()
    src = lax.rem(x + 4 - lax.div(slot - 1, 2), 4)
    behind = jnp.where(lax.rem(slot, 2) == 1, 1, jnp.where(src < x, 0, 2))
    return jnp.where(slot < 3, z * 4 + x - 4 * slot, (z - behind) * 4 + src)


def active(slot, n1, n2):
    z, x = here()
    own = z * 4 + x
    low = start_of(own * ROWS, n1, n2) // ROWS
    return (block_of(slot) >= low) & (block_of(slot) < own) | (slot == 0)


def key_norms(kv_ref, slots, base, n1, n2):
    def one(slot, best):
        k = kv_ref[slot - base, :ROWS].astype(jnp.float32)
        norm = jnp.sum(k * k, 1, keepdims=True)
        return jnp.where(active(slot, n1, n2), jnp.maximum(best, norm), best)

    return jnp.max(lax.fori_loop(*slots, one, jnp.zeros((ROWS, 1), jnp.float32)))


def make_queries(lin_ref, total_ref, gain_ref, q_ref):
    scale = lax.rsqrt(total_ref[...] / ALL_WIDE + 1e-06)
    scale = jnp.broadcast_to(scale, (DH, ROWS)).T
    norm = jnp.zeros((ROWS, 1), jnp.float32)
    for h in range(HEADS):
        gain = gain_ref[0:1, h * DH : (h + 1) * DH]
        q = (lin_ref[:, h * DH : (h + 1) * DH].astype(jnp.float32) * scale * gain).astype(jnp.bfloat16)
        wide = q.astype(jnp.float32)
        norm = jnp.maximum(norm, jnp.sum(wide * wide, 1, keepdims=True))
        q_ref[h, :, :DH] = q
        q_ref[h, :, DH:] = jnp.zeros((ROWS, DH), jnp.bfloat16)
    return jnp.max(norm)


def ones_beside(v):
    return jnp.concatenate([v, jnp.ones((ROWS, DH), jnp.bfloat16)], 1)


def bounded_tile(kv_ref, slot, base, begin_first, q_ref, acc_ref):
    kk = jnp.concatenate([kv_ref[slot - base, :ROWS]] * 2, 1)
    key = block_of(slot) * ROWS + lax.broadcasted_iota(jnp.int32, (ROWS, 256), 0)
    inside = (key >= begin_first).astype(jnp.float32).astype(jnp.bfloat16)
    v = ones_beside(kv_ref[slot - base, ROWS:]) * inside
    for h in range(HEADS):
        p = jnp.exp2(dot(q_ref[h], kk, NT)).astype(jnp.bfloat16)
        acc_ref[h] += dot(p, v)


def make_mask(mask_ref, block, first, begin):
    row = lax.broadcasted_iota(jnp.int32, (ROWS, ROWS), 0)
    key = block * ROWS + lax.broadcasted_iota(jnp.int32, (ROWS, ROWS), 1)
    mask_ref[...] = jnp.where((key >= begin) & (key <= first + row), 0.0, FAR)


def any_tile(kv_ref, slot, base, first, begin, q_ref, acc_ref, mask_ref, top_ref):
    make_mask(mask_ref, block_of(slot), first, begin)
    kk = jnp.concatenate([kv_ref[slot - base, :ROWS]] * 2, 1)
    v = ones_beside(kv_ref[slot - base, ROWS:])

    def head(h, carry):
        s = jnp.maximum(dot(q_ref[h], kk, NT) * FACTOR + mask_ref[...], FAR)
        old = top_ref[h]
        new = jnp.maximum(old, jnp.max(s, 1, keepdims=True))
        p = jnp.exp2(s - jnp.concatenate([new] * 4, 1)).astype(jnp.bfloat16)
        fade = jnp.exp2(old - new)
        acc_ref[h] = acc_ref[h] * jnp.concatenate([fade] * 2, 1) + dot(p, v)
        top_ref[h] = new
        return carry

    lax.fori_loop(0, HEADS, head, 0)


def in_softmax_phase():
    return lax.axis_index("phase") == 1


def rows_of():
    z, x = here()
    first = (z * 4 + x) * ROWS
    return first, first + lax.broadcasted_iota(jnp.int32, (ROWS, 1), 0)


def open_kernel(n_ref, lin_ref, total_ref, gain_ref, near_hbm, far_hbm, q_ref, acc_ref, top_hbm, stat_ref, kv_ref, mask_ref, top_ref, sems):
    @pl.when(in_softmax_phase())
    def _():
        n1, n2 = n_ref[0], n_ref[1]
        first, positions = rows_of()
        copies = [pltpu.make_async_copy(src, kv_ref.at[i], sems.at[i]) for i, src in enumerate((near_hbm, far_hbm))]
        for copy in copies:
            copy.start()
        q_most = make_queries(lin_ref, total_ref, gain_ref, q_ref)
        acc_ref[...] = jnp.zeros_like(acc_ref)
        for copy in copies:
            copy.wait()
        safe = q_most * key_norms(kv_ref, (1, 3), 1, n1, n2) < (SAFE / FACTOR) ** 2
        stat_ref[0] = q_most
        stat_ref[1] = jnp.where(safe, 1.0, 0.0)

        @pl.when(safe)
        def _():
            for h in range(HEADS):
                hi, lo = split(q_ref[h, :, :DH].astype(jnp.float32) * FACTOR)
                q_ref[h, :, :DH] = hi
                q_ref[h, :, DH:] = lo
            begin_first = start_of(first, n1, n2)

            def step(slot, carry):
                pl.when(active(slot, n1, n2))(lambda: bounded_tile(kv_ref, slot, 1, begin_first, q_ref, acc_ref))
                return carry

            lax.fori_loop(1, 3, step, 0)

        @pl.when(jnp.logical_not(safe))
        def _():
            top_ref[...] = jnp.full(top_ref.shape, FAR, jnp.float32)
            begin = start_of(positions, n1, n2)

            def step(slot, carry):
                pl.when(active(slot, n1, n2))(
                    lambda: any_tile(kv_ref, slot, 1, first, begin, q_ref, acc_ref, mask_ref, top_ref)
                )
                return carry

            lax.fori_loop(1, 3, step, 0)
            copy = pltpu.make_async_copy(top_ref, top_hbm, sems.at[0])
            copy.start()
            copy.wait()


def close_kernel(n_ref, stat_ref, lin_ref, total_ref, gain_ref, q_ref, part_ref, top_hbm, *refs):
    kv_hbm, (out_hbm, kv_ref, raw_ref, acc_ref, mask_ref, top_ref, out_ref, kv_sems, out_sems) = refs[:4], refs[4:]

    @pl.when(jnp.logical_not(in_softmax_phase()))
    def _():
        copy = pltpu.make_async_copy(lin_ref, out_hbm, out_sems.at[0])
        copy.start()
        copy.wait()

    @pl.when(in_softmax_phase())
    def _():
        close(
            n_ref, stat_ref, lin_ref, total_ref, gain_ref, q_ref, part_ref, top_hbm, kv_hbm,
            out_hbm, kv_ref, raw_ref, acc_ref, mask_ref, top_ref, out_ref, kv_sems, out_sems,
        )


def close(
    n_ref, stat_ref, lin_ref, total_ref, gain_ref, q_ref, part_ref, top_hbm, kv_hbm,
    out_hbm, kv_ref, raw_ref, acc_ref, mask_ref, top_ref, out_ref, kv_sems, out_sems,
):
    n1, n2 = n_ref[0], n_ref[1]
    first, positions = rows_of()
    begin_first = start_of(first, n1, n2)
    begin = start_of(positions, n1, n2)
    base = 2

    def fetch(slot):
        if slot == 0:
            return pltpu.make_async_copy(kv_hbm[0], kv_ref.at[0], kv_sems.at[0])
        src = kv_hbm[(slot - 1) // 2].at[pl.ds((slot - 1) % 2 * 2 * ROWS, 2 * ROWS)]
        return pltpu.make_async_copy(src, kv_ref.at[slot - base], kv_sems.at[slot - base])

    here_slots = (0,) + tuple(range(3, SLOTS))
    for slot in here_slots:
        pl.when(active(slot, n1, n2))(lambda: fetch(slot).start())
    acc_ref[...] = part_ref[...]
    for slot in here_slots:
        pl.when(active(slot, n1, n2))(lambda: fetch(slot).wait())

    k_most = jnp.maximum(key_norms(kv_ref, (3, SLOTS), base, n1, n2), key_norms(kv_ref, (0, 1), 0, n1, n2))
    opened_safe = stat_ref[1] > 0.5
    safe = opened_safe & (stat_ref[0] * k_most < (SAFE / FACTOR) ** 2)

    @pl.when(safe)
    def _():
        def step(slot, carry):
            pl.when(active(slot, n1, n2))(lambda: bounded_tile(kv_ref, slot, base, begin_first, q_ref, acc_ref))
            return carry

        lax.fori_loop(3, SLOTS, step, 0)

        make_mask(mask_ref, block_of(0), first, begin)
        kk = jnp.concatenate([kv_ref[0, :ROWS]] * 2, 1)
        v = ones_beside(kv_ref[0, ROWS:])
        keep = (begin < first).astype(jnp.float32)
        half = ROWS // 2
        for h in range(HEADS):
            for r in range(2):
                rows, span = slice(r * half, (r + 1) * half), (r + 1) * half
                s = dot(q_ref[h, rows, :], kk[:span], NT) + mask_ref[rows, :span]
                p = jnp.exp2(s).astype(jnp.bfloat16)
                acc_ref[h, rows, :] = acc_ref[h, rows, :] * keep[rows] + dot(p, v[:span])

    @pl.when(jnp.logical_not(safe))
    def _():
        make_queries(lin_ref, total_ref, gain_ref, raw_ref)

        @pl.when(jnp.logical_not(opened_safe))
        def _():
            copy = pltpu.make_async_copy(top_hbm, top_ref, kv_sems.at[0])
            copy.start()
            copy.wait()

        @pl.when(opened_safe)
        def _():
            opened = active(1, n1, n2) | active(2, n1, n2)
            keep = (positions - first < jnp.where(opened, ROWS, 0)) & (begin == begin_first)
            for h in range(HEADS):
                top_ref[h] = jnp.where(jnp.broadcast_to(keep, (ROWS, DH)), 0.0, FAR)
                acc_ref[h] = jnp.where(jnp.broadcast_to(keep, (ROWS, 256)), acc_ref[h], 0.0)

        def step(slot, carry):
            pl.when(active(slot, n1, n2))(
                lambda: any_tile(kv_ref, slot, base, first, begin, raw_ref, acc_ref, mask_ref, top_ref)
            )
            return carry

        lax.fori_loop(3, SLOTS, step, 0)
        any_tile(kv_ref, 0, 0, first, begin, raw_ref, acc_ref, mask_ref, top_ref)

    copies = []
    for h in range(HEADS):
        lanes = slice(h * DH, (h + 1) * DH)
        out_ref[:, lanes] = (acc_ref[h, :, :DH] / acc_ref[h, :, DH:]).astype(jnp.bfloat16)
        copies.append(pltpu.make_async_copy(out_ref.at[:, lanes], out_hbm.at[:, lanes], out_sems.at[h]))
        copies[-1].start()
    for copy in copies:
        copy.wait()


VMEM = pl.BlockSpec(memory_space=pltpu.VMEM)
SMEM = pl.BlockSpec(memory_space=pltpu.SMEM)
ANY = pl.BlockSpec(memory_space=pl.ANY)


def call(kernel, outs, out_specs, args, in_specs, scratch, flops, limit):
    return pl.pallas_call(
        kernel,
        out_shape=tuple(outs),
        in_specs=in_specs,
        out_specs=tuple(out_specs),
        scratch_shapes=scratch,
        compiler_params=pltpu.CompilerParams(vmem_limit_bytes=limit << 20),
        cost_estimate=pl.CostEstimate(flops=flops, bytes_accessed=0, transcendentals=0),
    )(*args)


def shape(dims, dtype=jnp.float32):
    return jax.ShapeDtypeStruct(dims, dtype)


def row_sum(counts, parts):
    return call(row_sum_kernel, [shape((QUARTER, DH))], [VMEM], (counts,) + tuple(parts), [SMEM] + [VMEM] * 4, [], 0, 8)[0]


def priors_of(counts, parts, near, far):
    return call(
        prior_kernel,
        [shape((QUARTER, DH))] * 4,
        [VMEM] * 4,
        (counts,) + tuple(parts) + (near, far),
        [SMEM] + [VMEM] * 6,
        [],
        1000000000,
        8,
    )


def pack(own_kv, near_kv, far_kv):
    return call(
        pack_kernel,
        [shape((4 * ROWS, DH), own_kv.dtype)] * 3,
        [ANY] * 3,
        (own_kv, near_kv, far_kv),
        [ANY] * 3,
        [pltpu.SemaphoreType.DMA((6,))],
        5000000000,
        4,
    )


def states(doc_ids, key_feats, values, keys_soft, values_soft):
    bf16 = jnp.bfloat16
    return call(
        states_kernel,
        [shape((QUARTER, DH))] * 4 + [shape((2 * ROWS, DH), bf16), shape((8,), jnp.int32)],
        [VMEM] * 5 + [SMEM],
        (doc_ids.reshape(-1, DH), key_feats, values, keys_soft, values_soft),
        [ANY] * 5,
        [
            pltpu.VMEM((HEADS * FEATS, DH), jnp.float32),
            pltpu.VMEM((doc_ids.shape[0] // DH, DH), jnp.int32),
            pltpu.VMEM((ROWS, DH), bf16),
            pltpu.VMEM((ROWS, WIDE), bf16),
            pltpu.SemaphoreType.DMA((5,)),
        ],
        0,
        60,
    )


def local_part(counts, query_feats, key_feats, values):
    bf16 = jnp.bfloat16
    return call(
        local_kernel,
        [shape((ROWS, WIDE)), shape((ROWS, DH)), shape((ROWS, HEADS * 256), bf16), shape((ROWS, HEADS * 256), bf16)],
        [VMEM] * 4,
        (counts, query_feats, key_feats, values),
        [SMEM] + [VMEM] * 3,
        [pltpu.VMEM((ROWS, ROWS), jnp.float32)],
        0,
        24,
    )


def finish(counts, feats_hi, feats_lo, num, den, parts):
    return call(
        finish_kernel,
        [shape((ROWS, WIDE), jnp.bfloat16), shape((1, ROWS))],
        [VMEM] * 2,
        (counts, feats_hi, feats_lo, num, den) + tuple(parts),
        [SMEM] + [VMEM] * 8,
        [pltpu.VMEM((HEADS * FEATS, DH), jnp.float32)],
        8000000000,
        20,
    )


def soft_open(counts, linear_out, total, gain, near_kv, far_kv):
    bf16 = jnp.bfloat16
    return call(
        open_kernel,
        [shape((HEADS, ROWS, 256), bf16), shape((HEADS, ROWS, 256)), shape((HEADS, ROWS, DH)), shape((8,))],
        [VMEM, VMEM, ANY, SMEM],
        (counts, linear_out, total, gain, near_kv, far_kv),
        [SMEM] + [VMEM] * 3 + [ANY] * 2,
        [
            pltpu.VMEM((2, 2 * ROWS, DH), bf16),
            pltpu.VMEM((ROWS, ROWS), jnp.float32),
            pltpu.VMEM((HEADS, ROWS, DH), jnp.float32),
            pltpu.SemaphoreType.DMA((2,)),
        ],
        0,
        28,
    )


def soft_close(counts, stat, linear_out, total, gain, queries, part, top, pieces):
    bf16 = jnp.bfloat16
    return call(
        close_kernel,
        [shape((ROWS, WIDE), bf16)],
        [ANY],
        (counts, stat, linear_out, total, gain, queries, part, top) + tuple(pieces),
        [SMEM] * 2 + [VMEM] * 5 + [ANY] * 5,
        [
            pltpu.VMEM((SLOTS - 2, 2 * ROWS, DH), bf16),
            pltpu.VMEM((HEADS, ROWS, 256), bf16),
            pltpu.VMEM((HEADS, ROWS, 256), jnp.float32),
            pltpu.VMEM((ROWS, ROWS), jnp.float32),
            pltpu.VMEM((HEADS, ROWS, DH), jnp.float32),
            pltpu.VMEM((ROWS, WIDE), bf16),
            pltpu.SemaphoreType.DMA((SLOTS - 2,)),
            pltpu.SemaphoreType.DMA((HEADS,)),
        ],
        0,
        32,
    )[0]


def shift(x, axis, by):
    size = lax.axis_size(axis)
    return lax.ppermute(x, axis, [(i, (i + by) % size) for i in range(size)])


def after(x, *others):
    return lax.optimization_barrier((x,) + others)[0]


def local(query_feats, key_feats, values, keys_soft, values_soft, norm_gain, doc_ids):
    zs = lax.axis_size("z")
    *chunks, own_kv, counts = states(doc_ids, key_feats, values, keys_soft, values_soft)

    parts = [chunks[0]] + [shift(chunks[s], "x", s) for s in (1, 2, 3)]

    near_kv = lax.ppermute(own_kv, ("phase", "z"), [(zs + i, zs + i + 1) for i in range(zs - 1)])
    far_kv = lax.ppermute(own_kv, ("phase", "z"), [(i, zs + i + 2) for i in range(zs - 2)])

    local_sums = local_part(counts, query_feats, key_feats, values)
    total = row_sum(counts, parts)
    near = lax.ppermute(total, "z", [(i, i + 1) for i in range(zs - 1)])
    far = lax.ppermute(
        total,
        ("phase", "z"),
        [((1 - p) * zs + i, p * zs + i + 2) for p in range(2) for i in range(zs - 2)],
    )

    messages = lax.optimization_barrier((total,) + tuple(pack(own_kv, near_kv, far_kv)))[1:]
    others = [
        lax.ppermute(message, ("phase", "x"), [(4 + i, 4 + (i + s) % 4) for i in range(4)])
        for s, message in zip((1, 2, 3), messages)
    ]

    near = after(near, *local_sums)
    priors = priors_of(counts, parts, near, far)
    arrived = [priors[0]] + [shift(priors[s], "x", s) for s in (1, 2, 3)]
    num, den, feats_hi, feats_lo = local_sums
    linear_out, squares = finish(counts, feats_hi, feats_lo, num, den, arrived)
    total = squares + shift(squares, "core", 1)
    for pairs in ((1, 0, 3, 2), (3, 2, 1, 0)):
        total = total + lax.ppermute(total, "y", list(enumerate(pairs)))
    gain = norm_gain[None]
    queries, part, top, stat = soft_open(counts, linear_out, total, gain, near_kv, far_kv)
    return soft_close(counts, stat, linear_out, total, gain, queries, part, top, [own_kv] + others)[None]


def solution(mesh):
    fine = Mesh(mesh.devices.reshape(2, 4, 4, 4, 2), ("phase", "z", "x", "y", "core"))
    seq, head = ("z", "x"), ("y", "core")
    return jax.shard_map(
        local,
        mesh=fine,
        in_specs=(
            P(seq, head),
            P(seq, head),
            P(seq, head),
            P(seq, head),
            P(seq, head),
            P(head),
            P(),
        ),
        out_specs=P("phase", seq, head),
        check_vma=False,
    )
```

time: 741 us -> 118 us (0.16); the launches traced: 727 us -> 117 us
  waiting for transfers between devices: 396 us -> 13.9 us
  matrix products: 102 us -> 0 us
  Pallas kernels: 0 us -> 75.2 us
  local copies, waits for them, and re-layouts: 66.9 us -> 1.57 us
  other arithmetic: 60.2 us -> 0.01 us
  starting transfers between devices: 78.3 us -> 26.4 us
  blocking collectives: 12.6 us -> 0 us
  loops' own time: 10 us -> 0 us
    ppermute x61 -> x16, waiting for transfers between devices: 396 us -> 13.9 us  [the longest x7 7.02 us: shift(): return lax.ppermute(x, axis, [(i, (i + by) % size) for i in range(size)])]
    dot_general x32 -> x0, matrix products: 102 us -> none  [the longest x16 63.5 us: update(): jnp.einsum('kgcj,kjd->kgcd', expo.astype(jnp.bfloat16), value_heads, pref...]
    pallas_call x0 -> x8, Pallas kernels: none -> 75.2 us  [call(): pl.pallas_call(kernel, out_shape=tuple(outs), in_specs=in_specs, out_spec...]
    ppermute x61 -> x16, starting transfers between devices: 78.3 us -> 26.4 us  [the longest x3 10.3 us: local(): lax.ppermute(message, ('phase', 'x'), [(4 + i, 4 + (i + s) % 4) for i in...]
    reduce_sum x17 -> x0, other arithmetic: 32.8 us -> none  [the longest x16 32.5 us: update(): jnp.sum(expo, -1)]
    cond x83 -> x0, local copies, waits for them, and re-layouts: 22.7 us -> none
    while x90 -> x0, local copies, waits for them, and re-layouts: 21.8 us -> none
    add x77 -> x3, other arithmetic: 18.6 us -> 0.01 us  [the longest x2 0.01 us: local(): total = total + lax.ppermute(total, 'y', list(enumerate(pairs)))]
  transfers between devices with their start and end apart: 61 -> 16, of which waited for: 30 -> 7; matrix products, arithmetic and copies ran while one was open for 22% -> 0% of each run, Pallas kernels for 0% -> 17%
where the time goes in v1:
time: 118 us; the launch traced here: 117 us
  Pallas kernels  75.2 us (64%)
  starting transfers between devices  26.4 us (22%)
  waiting for transfers between devices  13.9 us (12%)
  local copies, waits for them, and re-layouts  1.57 us (1%)
    pallas_call x8, Pallas kernels, call(): pl.pallas_call(kernel, out_shape=tuple(outs), in_specs=in_specs, out_spec...  75.2 us
    ppermute x3, starting transfers between devices, local(): lax.ppermute(message, ('phase', 'x'), [(4 + i, 4 + (i + s) % 4) for i in...  10.3 us
    ppermute x7, waiting for transfers between devices, shift(): return lax.ppermute(x, axis, [(i, (i + by) % size) for i in range(size)])  7.02 us
    ppermute x7, starting transfers between devices, shift(): return lax.ppermute(x, axis, [(i, (i + by) % size) for i in range(size)])  6.29 us
    ppermute x2, starting transfers between devices, local(): total = total + lax.ppermute(total, 'y', list(enumerate(pairs)))  4.58 us
    ppermute x2, waiting for transfers between devices, local(): total = total + lax.ppermute(total, 'y', list(enumerate(pairs)))  3.8 us
    ppermute x1, waiting for transfers between devices, local(): lax.ppermute(total, ('phase', 'z'), [((1 - p) * zs + i, p * zs + i + 2) f...  3.1 us
  transfers between devices with their start and end apart: 16, of which 7 were waited for; matrix products, arithmetic and copies ran while one was open for 0% of the time, Pallas kernels for 17%

profile of v1, /device:TPU:230, one launch (start us, length us, event | category | flops | bytes accessed | tf_op | source)
XLA Modules:
  0.0 117.4 jit_solution(3301215017730374055)
XLA Ops:
  0.0 4.2 %shard_map.73 = (f32[320,128]{1,0:T(8,128)}, f32[320,128]{1,0:T(8,128)}, f32[320,128]{1,0:T(8,128)}, f32[320,128]{1,0:T(8,128)}, bf16[1024,128]{1,0:T(8,128)(2,1)}, /*index=5*/s32[8]{0:T(128)}) custom-call(s32[64,128]{1,0:T(8,128)} %bitcast.5, bf16[512,128]{1,0:T(8,128)(2,1)} %kf_ref.1, bf16[512,1024]{1,0:T(8,128)(2,1)} %v_ref.1, bf16[512,128]{1,0:T(8,128)(2,1)} %k_hbm.1, ...), custom_call_target="tpu_custom_call" | custom-call | tf_op jit(solution)/shard_map/pallas_call | solution.py:468
  4.7 2.4 %collective-permute-start.1 = (f32[320,128]{1,0:T(8,128)}, f32[320,128]{1,0:T(8,128)S(1)}, u32[]{:S(2)}, u32[]{:S(2)}) collective-permute-start(f32[320,128]{1,0:T(8,128)} %get-tuple-element.39), channel_id=1, source_target_pairs={{0,16},{8,24},{16,0},{24,8},{1,17},{9,25},{17,1},{25,9},{2,18},{10... | collective-permute-start | bytes 491528 | tf_op jit(solution)/shard_map/ppermute | solution.py:604
  7.2 1.3 %collective-permute-start.12 = (bf16[1024,128]{1,0:T(8,128)(2,1)}, bf16[1024,128]{1,0:T(8,128)(2,1)S(1)}, u32[]{:S(2)}, u32[]{:S(2)}) collective-permute-start(bf16[1024,128]{1,0:T(8,128)(2,1)} %get-tuple-element.48.own_hbm.refs_0_), channel_id=1, source_target_pairs={{0,192},{32,224},{1,193},{33,225},{2,194},{34,226},{3,195},{35,227... | collective-permute-start | bytes 786440 | tf_op jit(solution)/shard_map/ppermute | solution.py:618
  8.5 1.3 %collective-permute-start.11 = (bf16[1024,128]{1,0:T(8,128)(2,1)}, bf16[1024,128]{1,0:T(8,128)(2,1)S(1)}, u32[]{:S(2)}, u32[]{:S(2)}) collective-permute-start(bf16[1024,128]{1,0:T(8,128)(2,1)} %get-tuple-element.48.own_hbm.refs_0_), channel_id=1, source_target_pairs={{128,160},{160,192},{192,224},{129,161},{161,193},{193,225},{130,1... | collective-permute-start | bytes 786440 | tf_op jit(solution)/shard_map/ppermute | solution.py:617
  9.8 1.8 %collective-permute-done.p1_ref = f32[320,128]{1,0:T(8,128)S(1)} collective-permute-done((f32[320,128]{1,0:T(8,128)}, f32[320,128]{1,0:T(8,128)S(1)}, u32[]{:S(2)}, u32[]{:S(2)}) %collective-permute-start) | collective-permute-done | bytes 163872 | tf_op jit(solution)/shard_map/ppermute | solution.py:604
  11.6 2.0 %collective-permute-done.1.p2_ref = f32[320,128]{1,0:T(8,128)S(1)} collective-permute-done((f32[320,128]{1,0:T(8,128)}, f32[320,128]{1,0:T(8,128)S(1)}, u32[]{:S(2)}, u32[]{:S(2)}) %collective-permute-start.1) | collective-permute-done | bytes 163872 | tf_op jit(solution)/shard_map/ppermute | solution.py:604
  13.6 2.1 %collective-permute-done.2.p3_ref = f32[320,128]{1,0:T(8,128)S(1)} collective-permute-done((f32[320,128]{1,0:T(8,128)}, f32[320,128]{1,0:T(8,128)S(1)}, u32[]{:S(2)}, u32[]{:S(2)}) %collective-permute-start.2) | collective-permute-done | bytes 163872 | tf_op jit(solution)/shard_map/ppermute | solution.py:604
  15.6 0.9 copy-done.3
  17.8 1.3 %collective-permute-start.3 = (f32[320,128]{1,0:T(8,128)S(1)}, f32[320,128]{1,0:T(8,128)S(1)}, u32[]{:S(2)}, u32[]{:S(2)}) collective-permute-start(f32[320,128]{1,0:T(8,128)S(1)} %shard_map.75), channel_id=1, source_target_pairs={{0,32},{32,64},{64,96},{1,33},{33,65},{65,97},{2,34},{34,66},{66,9... | collective-permute-start | bytes 491528 | tf_op jit(solution)/shard_map/ppermute | solution.py:622
  19.1 1.3 %collective-permute-start.4 = (f32[320,128]{1,0:T(8,128)S(1)}, f32[320,128]{1,0:T(8,128)S(1)}, u32[]{:S(2)}, u32[]{:S(2)}) collective-permute-start(f32[320,128]{1,0:T(8,128)S(1)} %shard_map.75), channel_id=1, source_target_pairs={{128,64},{160,96},{0,192},{32,224},{129,65},{161,97},{1,193},{33,2... | collective-permute-start | bytes 491528 | tf_op jit(solution)/shard_map/ppermute | solution.py:623
  20.4 5.0 %shard_map.74 = (f32[512,1024]{1,0:T(8,128)S(1)}, f32[512,128]{1,0:T(8,128)S(1)}, bf16[512,2048]{1,0:T(8,128)(2,1)S(1)}, bf16[512,2048]{1,0:T(8,128)(2,1)S(1)}) custom-call(s32[8]{0:T(128)S(1)} %copy-done.7, bf16[512,128]{1,0:T(8,128)(2,1)S(1)} %copy-done.5, bf16[512,128]{1,0:T(8,128)(2,1)S(1)} %copy-done.1, bf16[512,1024]{1,0:T(8,128)(2,1)S(1)} %copy-done), custom_call_target="tpu_custom_call" | custom-call | tf_op jit(solution)/shard_map/pallas_call | solution.py:468
  25.5 3.1 %collective-permute-done.4.far_ref = f32[320,128]{1,0:T(8,128)S(1)} collective-permute-done((f32[320,128]{1,0:T(8,128)S(1)}, f32[320,128]{1,0:T(8,128)S(1)}, u32[]{:S(2)}, u32[]{:S(2)}) %collective-permute-start.4) | collective-permute-done | bytes 163872 | tf_op jit(solution)/shard_map/ppermute | solution.py:623
  30.2 2.0 %collective-permute-start.6 = (f32[320,128]{1,0:T(8,128)S(1)}, f32[320,128]{1,0:T(8,128)S(1)}, u32[]{:S(2)}, u32[]{:S(2)}) collective-permute-start(f32[320,128]{1,0:T(8,128)S(1)} %get-tuple-element.44), channel_id=1, source_target_pairs={{0,16},{8,24},{16,0},{24,8},{1,17},{9,25},{17,1},{25,9},{2,18},{10... | collective-permute-start | bytes 491528 | tf_op jit(solution)/shard_map/ppermute | solution.py:604
  32.8 4.8 %collective-permute-start.13 = (bf16[2048,128]{1,0:T(8,128)(2,1)S(1)}, bf16[2048,128]{1,0:T(8,128)(2,1)S(1)}, u32[]{:S(2)}, u32[]{:S(2)}) collective-permute-start(bf16[2048,128]{1,0:T(8,128)(2,1)S(1)} %get-tuple-element.56), channel_id=1, source_target_pairs={{128,136},{136,144},{144,152},{152,128},{129,137},{137,145},{145,1... | collective-permute-start | bytes 1572872 | tf_op jit(solution)/shard_map/ppermute | solution.py:631
  37.7 2.2 %collective-permute-start.14 = (bf16[2048,128]{1,0:T(8,128)(2,1)S(1)}, bf16[2048,128]{1,0:T(8,128)(2,1)S(1)}, u32[]{:S(2)}, u32[]{:S(2)}) collective-permute-start(bf16[2048,128]{1,0:T(8,128)(2,1)S(1)} %get-tuple-element.57), channel_id=1, source_target_pairs={{128,144},{136,152},{144,128},{152,136},{129,145},{137,153},{145,1... | collective-permute-start | bytes 1572872 | tf_op jit(solution)/shard_map/ppermute | solution.py:631
  39.9 3.3 %collective-permute-start.15 = (bf16[2048,128]{1,0:T(8,128)(2,1)S(1)}, bf16[2048,128]{1,0:T(8,128)(2,1)S(1)}, u32[]{:S(2)}, u32[]{:S(2)}) collective-permute-start(bf16[2048,128]{1,0:T(8,128)(2,1)S(1)} %get-tuple-element.58), channel_id=1, source_target_pairs={{128,152},{136,128},{144,136},{152,144},{129,153},{137,129},{145,1... | collective-permute-start | bytes 1572872 | tf_op jit(solution)/shard_map/ppermute | solution.py:631
  43.3 2.9 %shard_map.77 = (bf16[512,1024]{1,0:T(8,128)(2,1)S(1)}, f32[1,512]{1,0:T(1,128)S(1)}) custom-call(s32[8]{0:T(128)S(1)} %copy-done.8, bf16[512,2048]{1,0:T(8,128)(2,1)S(1)} %get-tuple-element.33.hi_ref, bf16[512,2048]{1,0:T(8,128)(2,1)S(1)} %get-tuple-element.34.lo_ref, f32[512,1024]{1,0:T(8,128)S(1)} %get-tuple-element.35.num_ref, ...), custom_call_target="tpu_custom_call" | custom-call | flops 8000000000 | tf_op jit(solution)/shard_map/pallas_call | solution.py:468
  46.3 1.1 collective-permute-done.8
  47.4 1.6 %collective-permute-start.9 = (f32[1,512]{1,0:T(1,128)S(1)}, f32[1,512]{1,0:T(1,128)S(1)}, u32[]{:S(2)}, u32[]{:S(2)}) collective-permute-start(f32[1,512]{1,0:T(1,128)S(1)} %add.9), channel_id=1, source_target_pairs={{0,2},{2,0},{4,6},{6,4},{1,3},{3,1},{5,7},{7,5},{8,10},{10,8},{12,... | collective-permute-start | bytes 6152 | tf_op jit(solution)/shard_map/ppermute | solution.py:642
  49.0 2.0 %collective-permute-done.9 = f32[1,512]{1,0:T(1,128)S(1)} collective-permute-done((f32[1,512]{1,0:T(1,128)S(1)}, f32[1,512]{1,0:T(1,128)S(1)}, u32[]{:S(2)}, u32[]{:S(2)}) %collective-permute-start.9) | collective-permute-done | bytes 2080 | tf_op jit(solution)/shard_map/ppermute | solution.py:642
  51.0 3.0 %collective-permute-start.10 = (f32[1,512]{1,0:T(1,128)S(1)}, f32[1,512]{1,0:T(1,128)S(1)}, u32[]{:S(2)}, u32[]{:S(2)}) collective-permute-start(f32[1,512]{1,0:T(1,128)S(1)} %add.10), channel_id=1, source_target_pairs={{0,6},{2,4},{4,2},{6,0},{1,7},{3,5},{5,3},{7,1},{8,14},{10,12},{12... | collective-permute-start | bytes 6152 | tf_op jit(solution)/shard_map/ppermute | solution.py:642
  54.0 1.8 %collective-permute-done.10 = f32[1,512]{1,0:T(1,128)S(1)} collective-permute-done((f32[1,512]{1,0:T(1,128)S(1)}, f32[1,512]{1,0:T(1,128)S(1)}, u32[]{:S(2)}, u32[]{:S(2)}) %collective-permute-start.10) | collective-permute-done | bytes 2080 | tf_op jit(solution)/shard_map/ppermute | solution.py:642
  55.8 9.8 %shard_map.78 = (bf16[8,512,256]{2,1,0:T(8,128)(2,1)S(1)}, f32[8,512,256]{2,1,0:T(8,128)S(1)}, f32[8,512,128]{2,1,0:T(8,128)S(1)}, f32[8]{0:T(128)S(1)}) custom-call(s32[8]{0:T(128)S(1)} %copy-done.8, bf16[512,1024]{1,0:T(8,128)(2,1)S(1)} %get-tuple-element.46.lin_ref, f32[1,512]{1,0:T(1,128)S(1)} %add.11.total_ref, f32[1,1024]{1,0:T(1,128)S(1)} %bitcast.3, ...), custom_call_target="tpu_custom_call" | custom-call | tf_op jit(solution)/shard_map/pallas_call | solution.py:468
  65.7 51.6 %shard_map.80 = bf16[512,1024]{1,0:T(8,128)(2,1)} custom-call(s32[8]{0:T(128)S(1)} %copy-done.8, f32[8]{0:T(128)S(1)} %get-tuple-element.49.stat_ref, bf16[512,1024]{1,0:T(8,128)(2,1)S(1)} %get-tuple-element.46.lin_ref, f32[1,512]{1,0:T(1,128)S(1)} %add.11.total_ref, f32[1,1024]{1,0:T(1,128)S(1)} %bitcast.4, ...), custom_call_target="tpu_custom_call" | custom-call | tf_op jit(solution)/shard_map/pallas_call | solution.py:468
  (37 shorter events, 4.1 us)
Async XLA Ops:
  0.0 20.4 %copy-start = (bf16[512,1024]{1,0:T(8,128)(2,1)S(1)}, bf16[512,1024]{1,0:T(8,128)(2,1)}, u32[]{:S(2)}) copy-start(bf16[512,1024]{1,0:T(8,128)(2,1)} %v_ref.1) | copy-start | bytes 3145732
  0.0 20.4 %copy-start.1 = (bf16[512,128]{1,0:T(8,128)(2,1)S(1)}, bf16[512,128]{1,0:T(8,128)(2,1)}, u32[]{:S(2)}) copy-start(bf16[512,128]{1,0:T(8,128)(2,1)} %kf_ref.1) | copy-start | bytes 393220
  0.0 20.4 %copy-start.5 = (bf16[512,128]{1,0:T(8,128)(2,1)S(1)}, bf16[512,128]{1,0:T(8,128)(2,1)}, u32[]{:S(2)}) copy-start(bf16[512,128]{1,0:T(8,128)(2,1)} %qf_ref.1) | copy-start | bytes 393220
  4.2 7.4 %collective-permute-start = (f32[320,128]{1,0:T(8,128)}, f32[320,128]{1,0:T(8,128)S(1)}, u32[]{:S(2)}, u32[]{:S(2)}) collective-permute-start(f32[320,128]{1,0:T(8,128)} %get-tuple-element.38), channel_id=1, source_target_pairs={{0,8},{8,16},{16,24},{24,0},{1,9},{9,17},{17,25},{25,1},{2,10},{10... | collective-permute-start | bytes 491528 | tf_op jit(solution)/shard_map/ppermute | solution.py:604
  4.7 8.8 %collective-permute-start.1 = (f32[320,128]{1,0:T(8,128)}, f32[320,128]{1,0:T(8,128)S(1)}, u32[]{:S(2)}, u32[]{:S(2)}) collective-permute-start(f32[320,128]{1,0:T(8,128)} %get-tuple-element.39), channel_id=1, source_target_pairs={{0,16},{8,24},{16,0},{24,8},{1,17},{9,25},{17,1},{25,9},{2,18},{10... | collective-permute-start | bytes 491528 | tf_op jit(solution)/shard_map/ppermute | solution.py:604
  7.2 8.5 %collective-permute-start.2 = (f32[320,128]{1,0:T(8,128)}, f32[320,128]{1,0:T(8,128)S(1)}, u32[]{:S(2)}, u32[]{:S(2)}) collective-permute-start(f32[320,128]{1,0:T(8,128)} %get-tuple-element.40), channel_id=1, source_target_pairs={{0,24},{8,0},{16,8},{24,16},{1,25},{9,1},{17,9},{25,17},{2,26},{10... | collective-permute-start | bytes 491528 | tf_op jit(solution)/shard_map/ppermute | solution.py:604
  7.2 25.4 %collective-permute-start.12 = (bf16[1024,128]{1,0:T(8,128)(2,1)}, bf16[1024,128]{1,0:T(8,128)(2,1)S(1)}, u32[]{:S(2)}, u32[]{:S(2)}) collective-permute-start(bf16[1024,128]{1,0:T(8,128)(2,1)} %get-tuple-element.48.own_hbm.refs_0_), channel_id=1, source_target_pairs={{0,192},{32,224},{1,193},{33,225},{2,194},{34,226},{3,195},{35,227... | collective-permute-start | bytes 786440 | tf_op jit(solution)/shard_map/ppermute | solution.py:618
  8.5 24.1 %collective-permute-start.11 = (bf16[1024,128]{1,0:T(8,128)(2,1)}, bf16[1024,128]{1,0:T(8,128)(2,1)S(1)}, u32[]{:S(2)}, u32[]{:S(2)}) collective-permute-start(bf16[1024,128]{1,0:T(8,128)(2,1)} %get-tuple-element.48.own_hbm.refs_0_), channel_id=1, source_target_pairs={{128,160},{160,192},{192,224},{129,161},{161,193},{193,225},{130,1... | collective-permute-start | bytes 786440 | tf_op jit(solution)/shard_map/ppermute | solution.py:617
  15.6 0.9 copy-start.3
  17.2 11.4 %copy-start.4 = (f32[320,128]{1,0:T(8,128)S(1)}, f32[320,128]{1,0:T(8,128)}, u32[]{:S(2)}) copy-start(f32[320,128]{1,0:T(8,128)} %get-tuple-element.37.p0_ref) | copy-start | bytes 491524
  17.8 7.7 %collective-permute-start.3 = (f32[320,128]{1,0:T(8,128)S(1)}, f32[320,128]{1,0:T(8,128)S(1)}, u32[]{:S(2)}, u32[]{:S(2)}) collective-permute-start(f32[320,128]{1,0:T(8,128)S(1)} %shard_map.75), channel_id=1, source_target_pairs={{0,32},{32,64},{64,96},{1,33},{33,65},{65,97},{2,34},{34,66},{66,9... | collective-permute-start | bytes 491528 | tf_op jit(solution)/shard_map/ppermute | solution.py:622
  19.1 9.5 %collective-permute-start.4 = (f32[320,128]{1,0:T(8,128)S(1)}, f32[320,128]{1,0:T(8,128)S(1)}, u32[]{:S(2)}, u32[]{:S(2)}) collective-permute-start(f32[320,128]{1,0:T(8,128)S(1)} %shard_map.75), channel_id=1, source_target_pairs={{128,64},{160,96},{0,192},{32,224},{129,65},{161,97},{1,193},{33,2... | collective-permute-start | bytes 491528 | tf_op jit(solution)/shard_map/ppermute | solution.py:623
  25.5 7.1 %copy-start.2 = (bf16[1024,128]{1,0:T(8,128)(2,1)S(1)}, bf16[1024,128]{1,0:T(8,128)(2,1)}, u32[]{:S(2)}) copy-start(bf16[1024,128]{1,0:T(8,128)(2,1)} %get-tuple-element.48.own_hbm.refs_0_) | copy-start | bytes 786436
  29.4 10.5 %collective-permute-start.5 = (f32[320,128]{1,0:T(8,128)S(1)}, f32[320,128]{1,0:T(8,128)S(1)}, u32[]{:S(2)}, u32[]{:S(2)}) collective-permute-start(f32[320,128]{1,0:T(8,128)S(1)} %get-tuple-element.43), channel_id=1, source_target_pairs={{0,8},{8,16},{16,24},{24,0},{1,9},{9,17},{17,25},{25,1},{2,10},{10... | collective-permute-start | bytes 491528 | tf_op jit(solution)/shard_map/ppermute | solution.py:604
  30.2 13.0 %collective-permute-start.6 = (f32[320,128]{1,0:T(8,128)S(1)}, f32[320,128]{1,0:T(8,128)S(1)}, u32[]{:S(2)}, u32[]{:S(2)}) collective-permute-start(f32[320,128]{1,0:T(8,128)S(1)} %get-tuple-element.44), channel_id=1, source_target_pairs={{0,16},{8,24},{16,0},{24,8},{1,17},{9,25},{17,1},{25,9},{2,18},{10... | collective-permute-start | bytes 491528 | tf_op jit(solution)/shard_map/ppermute | solution.py:604
  32.3 10.9 %copy-start.8 = (s32[8]{0:T(128)S(1)}, s32[8]{0:T(128)}, u32[]{:S(2)}) copy-start(s32[8]{0:T(128)} %get-tuple-element.32.n_ref) | copy-start | bytes 100
  32.3 10.9 %collective-permute-start.7 = (f32[320,128]{1,0:T(8,128)S(1)}, f32[320,128]{1,0:T(8,128)S(1)}, u32[]{:S(2)}, u32[]{:S(2)}) collective-permute-start(f32[320,128]{1,0:T(8,128)S(1)} %get-tuple-element.45), channel_id=1, source_target_pairs={{0,24},{8,0},{16,8},{24,16},{1,25},{9,1},{17,9},{25,17},{2,26},{10... | collective-permute-start | bytes 491528 | tf_op jit(solution)/shard_map/ppermute | solution.py:604
  32.8 32.8 %collective-permute-start.13 = (bf16[2048,128]{1,0:T(8,128)(2,1)S(1)}, bf16[2048,128]{1,0:T(8,128)(2,1)S(1)}, u32[]{:S(2)}, u32[]{:S(2)}) collective-permute-start(bf16[2048,128]{1,0:T(8,128)(2,1)S(1)} %get-tuple-element.56), channel_id=1, source_target_pairs={{128,136},{136,144},{144,152},{152,128},{129,137},{137,145},{145,1... | collective-permute-start | bytes 1572872 | tf_op jit(solution)/shard_map/ppermute | solution.py:631
  37.7 28.0 %collective-permute-start.14 = (bf16[2048,128]{1,0:T(8,128)(2,1)S(1)}, bf16[2048,128]{1,0:T(8,128)(2,1)S(1)}, u32[]{:S(2)}, u32[]{:S(2)}) collective-permute-start(bf16[2048,128]{1,0:T(8,128)(2,1)S(1)} %get-tuple-element.57), channel_id=1, source_target_pairs={{128,144},{136,152},{144,128},{152,136},{129,145},{137,153},{145,1... | collective-permute-start | bytes 1572872 | tf_op jit(solution)/shard_map/ppermute | solution.py:631
  39.9 25.8 %collective-permute-start.15 = (bf16[2048,128]{1,0:T(8,128)(2,1)S(1)}, bf16[2048,128]{1,0:T(8,128)(2,1)S(1)}, u32[]{:S(2)}, u32[]{:S(2)}) collective-permute-start(bf16[2048,128]{1,0:T(8,128)(2,1)S(1)} %get-tuple-element.58), channel_id=1, source_target_pairs={{128,152},{136,128},{144,136},{152,144},{129,153},{137,129},{145,1... | collective-permute-start | bytes 1572872 | tf_op jit(solution)/shard_map/ppermute | solution.py:631
  43.2 12.6 %copy-start.6 = (f32[1024]{0:T(1024)S(1)}, f32[1024]{0:T(1024)}, u32[]{:S(2)}) copy-start(f32[1024]{0:T(1024)} %param.12) | copy-start | bytes 12292
  46.2 1.2 %collective-permute-start.8 = (f32[1,512]{1,0:T(1,128)S(1)}, f32[1,512]{1,0:T(1,128)S(1)}, u32[]{:S(2)}, u32[]{:S(2)}) collective-permute-start(f32[1,512]{1,0:T(1,128)S(1)} %get-tuple-element.47), channel_id=1, source_target_pairs={{0,1},{1,0},{2,3},{3,2},{4,5},{5,4},{6,7},{7,6},{8,9},{9,8},{10,11... | collective-permute-start | bytes 6152 | tf_op jit(solution)/shard_map/ppermute | solution.py:604
  47.4 3.6 %collective-permute-start.9 = (f32[1,512]{1,0:T(1,128)S(1)}, f32[1,512]{1,0:T(1,128)S(1)}, u32[]{:S(2)}, u32[]{:S(2)}) collective-permute-start(f32[1,512]{1,0:T(1,128)S(1)} %add.9), channel_id=1, source_target_pairs={{0,2},{2,0},{4,6},{6,4},{1,3},{3,1},{5,7},{7,5},{8,10},{10,8},{12,... | collective-permute-start | bytes 6152 | tf_op jit(solution)/shard_map/ppermute | solution.py:642
  51.0 4.8 %collective-permute-start.10 = (f32[1,512]{1,0:T(1,128)S(1)}, f32[1,512]{1,0:T(1,128)S(1)}, u32[]{:S(2)}, u32[]{:S(2)}) collective-permute-start(f32[1,512]{1,0:T(1,128)S(1)} %add.10), channel_id=1, source_target_pairs={{0,6},{2,4},{4,2},{6,0},{1,7},{3,5},{5,3},{7,1},{8,14},{10,12},{12... | collective-permute-start | bytes 6152 | tf_op jit(solution)/shard_map/ppermute | solution.py:642
  (1 other events, 0.6 us)

commit v2 on v1

--- a/solution.py
+++ b/solution.py
@@ -19,7 +19,7 @@
 SLOTS = 9
 LOG2E = math.log2(math.e)
 FACTOR = LOG2E / math.sqrt(DH)
-SAFE = 110.0
+SAFE = 108.0
 FAR = -1e30
 
 NN = (((1,), (0,)), ((), ()))
@@ -60,10 +60,6 @@
     return lax.axis_index("z"), lax.axis_index("x")
 
 
-def row_block(x, s):
-    return lax.rem(x - s + 4, 4)
-
-
 def last_doc(block, n1, n2):
     return doc_of(block * ROWS + ROWS - 1, n1, n2)
 
@@ -72,17 +68,21 @@
     return x.astype(jnp.float32)
 
 
-def row_sum_kernel(n_ref, p0_ref, p1_ref, p2_ref, p3_ref, out_ref):
+def chunk_of(parts_ref, s):
+    return parts_ref[s * QUARTER : (s + 1) * QUARTER, :]
+
+
+def row_sum_kernel(n_ref, parts_ref, out_ref):
     n1, n2 = n_ref[0], n_ref[1]
     z, x = here()
     end = last_doc(z * 4 + 3, n1, n2)
     total = jnp.zeros((QUARTER, DH), jnp.float32)
-    for s, part in enumerate((p0_ref, p1_ref, p2_ref, p3_ref)):
-        total = total + flag(last_doc(z * 4 + row_block(x, s), n1, n2) == end) * part[...]
+    for s in range(4):
+        total = total + flag(last_doc(z * 4 + s, n1, n2) == end) * chunk_of(parts_ref, s)
     out_ref[...] = total
 
 
-def prior_kernel(n_ref, p0_ref, p1_ref, p2_ref, p3_ref, near_ref, far_ref, *outs):
+def prior_kernel(n_ref, parts_ref, near_ref, far_ref, *outs):
     n1, n2 = n_ref[0], n_ref[1]
     z, x = here()
     before = last_doc(z * 4 - 1, n1, n2)
@@ -91,9 +91,9 @@
         target = lax.rem(x + t, 4)
         doc = last_doc(z * 4 + target - 1, n1, n2)
         prior = flag(before == doc) * incoming
-        for s, part in enumerate((p0_ref, p1_ref, p2_ref, p3_ref)):
-            block = row_block(x, s)
-            prior = prior + flag((block < target) & (last_doc(z * 4 + block, n1, n2) == doc)) * part[...]
+        for s in range(4):
+            use = (s < target) & (last_doc(z * 4 + s, n1, n2) == doc)
+            prior = prior + flag(use) * chunk_of(parts_ref, s)
         out[...] = prior
 
 
@@ -110,7 +110,7 @@
         pltpu.make_async_copy(own_hbm, out.at[lower], sems.at[3 + s]).wait()
 
 
-def states_kernel(doc_hbm, kf_hbm, v_hbm, k_hbm, vs_hbm, c0_ref, c1_ref, c2_ref, c3_ref, kv_ref, n_ref, state_ref, doc_ref, kf_ref, v_ref, sems):
+def states_kernel(doc_hbm, kf_hbm, v_hbm, k_hbm, vs_hbm, state_ref, kv_ref, n_ref, doc_ref, kf_ref, v_ref, sems):
     pairs = [(doc_hbm, doc_ref), (kf_hbm, kf_ref), (v_hbm, v_ref), (k_hbm, kv_ref.at[:ROWS]), (vs_hbm, kv_ref.at[ROWS:])]
     copies = [pltpu.make_async_copy(src, dst, sems.at[i]) for i, (src, dst) in enumerate(pairs)]
     for copy in copies:
@@ -146,9 +146,6 @@
         base = h * FEATS + USED
         state_ref[base : base + 1, :] = across[h : h + 1, :DH]
         state_ref[base + 1 : base + 2, : FEATS - DH] = across[h : h + 1, DH:]
-    for s, out in enumerate((c0_ref, c1_ref, c2_ref, c3_ref)):
-        chunk = lax.rem(x + s, 4)
-        out[...] = state_ref[pl.ds(pl.multiple_of(chunk * QUARTER, QUARTER), QUARTER), :]
     copies[3].wait()
     copies[4].wait()
 
@@ -223,7 +220,7 @@
         out_ref[:, h * DH : (h + 1) * DH] = out
         wide = out.astype(jnp.float32)
         squares = squares + wide * wide
-    sq_ref[...] = jnp.sum(squares.T, 0, keepdims=True)
+    sq_ref[...] = jnp.broadcast_to(jnp.sum(squares.T, 0, keepdims=True), (8, ROWS))
 
 
 def block_of(slot):
@@ -240,24 +237,26 @@
     return (block_of(slot) >= low) & (block_of(slot) < own) | (slot == 0)
 
 
+def row_norms(x):
+    return dot((x * x).astype(jnp.bfloat16), jnp.ones((DH, DH), jnp.bfloat16))
+
+
 def key_norms(kv_ref, slots, base, n1, n2):
     def one(slot, best):
-        k = kv_ref[slot - base, :ROWS].astype(jnp.float32)
-        norm = jnp.sum(k * k, 1, keepdims=True)
+        norm = row_norms(kv_ref[slot - base, :ROWS].astype(jnp.float32))
         return jnp.where(active(slot, n1, n2), jnp.maximum(best, norm), best)
 
-    return jnp.max(lax.fori_loop(*slots, one, jnp.zeros((ROWS, 1), jnp.float32)))
+    return jnp.max(lax.fori_loop(*slots, one, jnp.zeros((ROWS, DH), jnp.float32)))
 
 
 def make_queries(lin_ref, total_ref, gain_ref, q_ref):
-    scale = lax.rsqrt(total_ref[...] / ALL_WIDE + 1e-06)
+    scale = lax.rsqrt(jnp.sum(total_ref[...], 0, keepdims=True) / ALL_WIDE + 1e-06)
     scale = jnp.broadcast_to(scale, (DH, ROWS)).T
-    norm = jnp.zeros((ROWS, 1), jnp.float32)
+    norm = jnp.zeros((ROWS, DH), jnp.float32)
     for h in range(HEADS):
         gain = gain_ref[0:1, h * DH : (h + 1) * DH]
         q = (lin_ref[:, h * DH : (h + 1) * DH].astype(jnp.float32) * scale * gain).astype(jnp.bfloat16)
-        wide = q.astype(jnp.float32)
-        norm = jnp.maximum(norm, jnp.sum(wide * wide, 1, keepdims=True))
+        norm = jnp.maximum(norm, row_norms(q.astype(jnp.float32)))
         q_ref[h, :, :DH] = q
         q_ref[h, :, DH:] = jnp.zeros((ROWS, DH), jnp.bfloat16)
     return jnp.max(norm)
@@ -272,9 +271,10 @@
     key = block_of(slot) * ROWS + lax.broadcasted_iota(jnp.int32, (ROWS, 256), 0)
     inside = (key >= begin_first).astype(jnp.float32).astype(jnp.bfloat16)
     v = ones_beside(kv_ref[slot - base, ROWS:]) * inside
-    for h in range(HEADS):
-        p = jnp.exp2(dot(q_ref[h], kk, NT)).astype(jnp.bfloat16)
-        acc_ref[h] += dot(p, v)
+    for h in range(0, HEADS, 2):
+        q = q_ref[h : h + 2].reshape(2 * ROWS, 256)
+        p = jnp.exp2(dot(q, kk, NT)).astype(jnp.bfloat16)
+        acc_ref[h : h + 2] += dot(p, v).reshape(2, ROWS, 256)
 
 
 def make_mask(mask_ref, block, first, begin):
@@ -481,7 +481,7 @@
 
 
 def row_sum(counts, parts):
-    return call(row_sum_kernel, [shape((QUARTER, DH))], [VMEM], (counts,) + tuple(parts), [SMEM] + [VMEM] * 4, [], 0, 8)[0]
+    return call(row_sum_kernel, [shape((QUARTER, DH))], [VMEM], (counts, parts), [SMEM, VMEM], [], 0, 8)[0]
 
 
 def priors_of(counts, parts, near, far):
@@ -489,8 +489,8 @@
         prior_kernel,
         [shape((QUARTER, DH))] * 4,
         [VMEM] * 4,
-        (counts,) + tuple(parts) + (near, far),
-        [SMEM] + [VMEM] * 6,
+        (counts, parts, near, far),
+        [SMEM] + [VMEM] * 3,
         [],
         1000000000,
         8,
@@ -514,12 +514,11 @@
     bf16 = jnp.bfloat16
     return call(
         states_kernel,
-        [shape((QUARTER, DH))] * 4 + [shape((2 * ROWS, DH), bf16), shape((8,), jnp.int32)],
-        [VMEM] * 5 + [SMEM],
+        [shape((HEADS * FEATS, DH)), shape((2 * ROWS, DH), bf16), shape((8,), jnp.int32)],
+        [VMEM] * 2 + [SMEM],
         (doc_ids.reshape(-1, DH), key_feats, values, keys_soft, values_soft),
         [ANY] * 5,
         [
-            pltpu.VMEM((HEADS * FEATS, DH), jnp.float32),
             pltpu.VMEM((doc_ids.shape[0] // DH, DH), jnp.int32),
             pltpu.VMEM((ROWS, DH), bf16),
             pltpu.VMEM((ROWS, WIDE), bf16),
@@ -547,7 +546,7 @@
 def finish(counts, feats_hi, feats_lo, num, den, parts):
     return call(
         finish_kernel,
-        [shape((ROWS, WIDE), jnp.bfloat16), shape((1, ROWS))],
+        [shape((ROWS, WIDE), jnp.bfloat16), shape((8, ROWS))],
         [VMEM] * 2,
         (counts, feats_hi, feats_lo, num, den) + tuple(parts),
         [SMEM] + [VMEM] * 8,
@@ -610,9 +609,9 @@
 
 def local(query_feats, key_feats, values, keys_soft, values_soft, norm_gain, doc_ids):
     zs = lax.axis_size("z")
-    *chunks, own_kv, counts = states(doc_ids, key_feats, values, keys_soft, values_soft)
-
-    parts = [chunks[0]] + [shift(chunks[s], "x", s) for s in (1, 2, 3)]
+    state, own_kv, counts = states(doc_ids, key_feats, values, keys_soft, values_soft)
+
+    parts = lax.all_to_all(state, "x", 0, 0, tiled=True)
 
     near_kv = lax.ppermute(own_kv, ("phase", "z"), [(zs + i, zs + i + 1) for i in range(zs - 1)])
     far_kv = lax.ppermute(own_kv, ("phase", "z"), [(i, zs + i + 2) for i in range(zs - 2)])
@@ -637,9 +636,7 @@
     arrived = [priors[0]] + [shift(priors[s], "x", s) for s in (1, 2, 3)]
     num, den, feats_hi, feats_lo = local_sums
     linear_out, squares = finish(counts, feats_hi, feats_lo, num, den, arrived)
-    total = squares + shift(squares, "core", 1)
-    for pairs in ((1, 0, 3, 2), (3, 2, 1, 0)):
-        total = total + lax.ppermute(total, "y", list(enumerate(pairs)))
+    total = lax.all_to_all(squares, ("y", "core"), 0, 0, tiled=True)
     gain = norm_gain[None]
     queries, part, top, stat = soft_open(counts, linear_out, total, gain, near_kv, far_kv)
     return soft_close(counts, stat, linear_out, total, gain, queries, part, top, [own_kv] + others)[None]

time: 118 us -> 131 us (1.11)
  the two profiles are of different devices: /device:TPU:230 before, /device:TPU:225 now
where the time goes in v2:
time: 131 us; the launch traced here: 130 us
  Pallas kernels  84 us (64%)
  starting transfers between devices  22.1 us (17%)
  blocking collectives  13.8 us (11%)
  waiting for transfers between devices  9.17 us (7%)
    pallas_call x8, Pallas kernels, call(): pl.pallas_call(kernel, out_shape=tuple(outs), in_specs=in_specs, out_spec...  84 us
    all_to_all x1, blocking collectives, local(): total = lax.all_to_all(squares, ('y', 'core'), 0, 0, tiled=True)  13.8 us
    ppermute x3, starting transfers between devices, local(): lax.ppermute(message, ('phase', 'x'), [(4 + i, 4 + (i + s) % 4) for i in...  10.1 us
    all_to_all x1, waiting for transfers between devices, local(): parts = lax.all_to_all(state, 'x', 0, 0, tiled=True)  7.38 us
    all_to_all x1, starting transfers between devices, local(): parts = lax.all_to_all(state, 'x', 0, 0, tiled=True)  4.02 us
    ppermute x3, starting transfers between devices, shift(): return lax.ppermute(x, axis, [(i, (i + by) % size) for i in range(size)])  2.85 us
  transfers between devices with their start and end apart: 11, of which 2 were waited for; matrix products, arithmetic and copies ran while one was open for 0% of the time, Pallas kernels for 21%

profile of v2, /device:TPU:225, one launch (start us, length us, event | category | flops | bytes accessed | tf_op | source)
XLA Modules:
  0.0 130.2 jit_solution(13136715558177070497)
XLA Ops:
  0.0 4.2 %shard_map.73 = (f32[1280,128]{1,0:T(8,128)}, bf16[1024,128]{1,0:T(8,128)(2,1)}, s32[8]{0:T(128)}) custom-call(s32[64,128]{1,0:T(8,128)} %bitcast.17, bf16[512,128]{1,0:T(8,128)(2,1)} %kf_ref.1, bf16[512,1024]{1,0:T(8,128)(2,1)} %v_ref.1, bf16[512,128]{1,0:T(8,128)(2,1)} %k_hbm.1, bf16[512,128]{1,0:T(8,128)(2,1)} %vs_hbm.1), custom_call_target="tpu_custom_call" | custom-call | tf_op jit(solution)/shard_map/pallas_call | solution.py:468
  4.2 4.0 %all-to-all-start = ((f32[4,320,128]{2,1,0:T(8,128)}), f32[4,320,128]{2,1,0:T(8,128)S(1)}, u32[]{:S(2)}, u32[]{:S(2)}) async-start(f32[4,320,128]{2,1,0:T(8,128)} %bitcast.16), calls=%async_computation | async-start | bytes 1310720 | tf_op jit(solution)/shard_map/all_to_all | solution.py:614
  8.2 1.3 collective-permute-start.6
  9.5 1.3 collective-permute-start.5
  10.8 7.4 %all-to-all-done = f32[4,320,128]{2,1,0:T(8,128)S(1)} async-done(((f32[4,320,128]{2,1,0:T(8,128)}), f32[4,320,128]{2,1,0:T(8,128)S(1)}, u32[]{:S(2)}, u32[]{:S(2)}) %all-to-all-start) | async-done | bytes 655392 | tf_op jit(solution)/shard_map/all_to_all | solution.py:614
  18.2 0.7 copy-done.5
  18.8 0.6 shard_map.75
  19.4 1.3 collective-permute-start
  20.7 1.3 collective-permute-start.1
  22.1 5.1 %shard_map.74 = (f32[512,1024]{1,0:T(8,128)S(1)}, f32[512,128]{1,0:T(8,128)S(1)}, bf16[512,2048]{1,0:T(8,128)(2,1)S(1)}, bf16[512,2048]{1,0:T(8,128)(2,1)S(1)}) custom-call(s32[8]{0:T(128)S(1)} %copy-done.6, bf16[512,128]{1,0:T(8,128)(2,1)S(1)} %copy-done.3, bf16[512,128]{1,0:T(8,128)(2,1)S(1)} %copy-done.1, bf16[512,1024]{1,0:T(8,128)(2,1)S(1)} %copy-done), custom_call_target="tpu_custom_call" | custom-call | tf_op jit(solution)/shard_map/pallas_call | solution.py:468
  27.2 1.8 %collective-permute-done.1.far_ref = f32[320,128]{1,0:T(8,128)S(1)} collective-permute-done((f32[320,128]{1,0:T(8,128)S(1)}, f32[320,128]{1,0:T(8,128)S(1)}, u32[]{:S(2)}, u32[]{:S(2)}) %collective-permute-start.1) | collective-permute-done | bytes 163872 | tf_op jit(solution)/shard_map/ppermute | solution.py:622
  29.0 0.8 shard_map.76
  29.8 0.4 collective-permute-start.2
  30.2 1.8 %collective-permute-start.3 = (f32[320,128]{1,0:T(8,128)S(1)}, f32[320,128]{1,0:T(8,128)S(1)}, u32[]{:S(2)}, u32[]{:S(2)}) collective-permute-start(f32[320,128]{1,0:T(8,128)S(1)} %get-tuple-element.38), channel_id=1, source_target_pairs={{0,16},{8,24},{16,0},{24,8},{1,17},{9,25},{17,1},{25,9},{2,18},{10... | collective-permute-start | bytes 491528 | tf_op jit(solution)/shard_map/ppermute | solution.py:603
  32.0 0.7 collective-permute-start.4
  32.7 0.2 shard_map.79
  32.9 2.7 %collective-permute-start.7 = (bf16[2048,128]{1,0:T(8,128)(2,1)S(1)}, bf16[2048,128]{1,0:T(8,128)(2,1)S(1)}, u32[]{:S(2)}, u32[]{:S(2)}) collective-permute-start(bf16[2048,128]{1,0:T(8,128)(2,1)S(1)} %get-tuple-element.50), channel_id=1, source_target_pairs={{128,136},{136,144},{144,152},{152,128},{129,137},{137,145},{145,1... | collective-permute-start | bytes 1572872 | tf_op jit(solution)/shard_map/ppermute | solution.py:630
  35.6 3.4 %collective-permute-start.8 = (bf16[2048,128]{1,0:T(8,128)(2,1)S(1)}, bf16[2048,128]{1,0:T(8,128)(2,1)S(1)}, u32[]{:S(2)}, u32[]{:S(2)}) collective-permute-start(bf16[2048,128]{1,0:T(8,128)(2,1)S(1)} %get-tuple-element.51), channel_id=1, source_target_pairs={{128,144},{136,152},{144,128},{152,136},{129,145},{137,153},{145,1... | collective-permute-start | bytes 1572872 | tf_op jit(solution)/shard_map/ppermute | solution.py:630
  39.0 4.0 %collective-permute-start.9 = (bf16[2048,128]{1,0:T(8,128)(2,1)S(1)}, bf16[2048,128]{1,0:T(8,128)(2,1)S(1)}, u32[]{:S(2)}, u32[]{:S(2)}) collective-permute-start(bf16[2048,128]{1,0:T(8,128)(2,1)S(1)} %get-tuple-element.52), channel_id=1, source_target_pairs={{128,152},{136,128},{144,136},{152,144},{129,153},{137,129},{145,1... | collective-permute-start | bytes 1572872 | tf_op jit(solution)/shard_map/ppermute | solution.py:630
  43.0 0.0 copy-start.4
  43.0 2.9 %shard_map.77 = (bf16[512,1024]{1,0:T(8,128)(2,1)S(1)}, f32[8,512]{1,0:T(8,128)S(1)}) custom-call(s32[8]{0:T(128)S(1)} %copy-done.6, bf16[512,2048]{1,0:T(8,128)(2,1)S(1)} %get-tuple-element.30.hi_ref, bf16[512,2048]{1,0:T(8,128)(2,1)S(1)} %get-tuple-element.31.lo_ref, f32[512,1024]{1,0:T(8,128)S(1)} %get-tuple-element.32.num_ref, ...), custom_call_target="tpu_custom_call" | custom-call | flops 8000000000 | tf_op jit(solution)/shard_map/pallas_call | solution.py:468
  45.9 13.8 %all_to_all.22 = f32[8,1,512]{2,1,0:T(1,128)S(1)} all-to-all(f32[8,1,512]{2,1,0:T(1,128)S(1)} %copy.8), channel_id=1, replica_groups=mesh['phase'=2,'z'=4,'x'=4,'y'=4,'core'=2] {'y','core'}, dimensions={0} | all-to-all | bytes 32768 | tf_op jit(solution)/shard_map/all_to_all | solution.py:639
  59.8 17.6 %shard_map.78 = (bf16[8,512,256]{2,1,0:T(8,128)(2,1)S(1)}, f32[8,512,256]{2,1,0:T(8,128)S(1)}, f32[8,512,128]{2,1,0:T(8,128)S(1)}, f32[8]{0:T(128)S(1)}) custom-call(s32[8]{0:T(128)S(1)} %copy-done.6, bf16[512,1024]{1,0:T(8,128)(2,1)S(1)} %get-tuple-element.40.lin_ref, f32[8,512]{1,0:T(8,128)S(1)} %bitcast.11, f32[1,1024]{1,0:T(1,128)S(1)} %bitcast.13, ...), custom_call_target="tpu_custom_call" | custom-call | tf_op jit(solution)/shard_map/pallas_call | solution.py:468
  77.4 52.6 %shard_map.80 = bf16[512,1024]{1,0:T(8,128)(2,1)} custom-call(s32[8]{0:T(128)S(1)} %copy-done.6, f32[8]{0:T(128)S(1)} %get-tuple-element.43.stat_ref, bf16[512,1024]{1,0:T(8,128)(2,1)S(1)} %get-tuple-element.40.lin_ref, f32[8,512]{1,0:T(8,128)S(1)} %bitcast.12, f32[1,1024]{1,0:T(1,128)S(1)} %bitcast.14, bf16[8,512,256]{2,1,0:T(8,128)(2,1)S(1)} %get-tuple-element.44.q_ref, ...), custom_call_target="tpu_custom_call" | custom-call | tf_op jit(solution)/shard_map/pallas_call | solution.py:468
  (23 shorter events, 0.1 us)
Async XLA Ops:
  0.0 22.1 %copy-start = (bf16[512,1024]{1,0:T(8,128)(2,1)S(1)}, bf16[512,1024]{1,0:T(8,128)(2,1)}, u32[]{:S(2)}) copy-start(bf16[512,1024]{1,0:T(8,128)(2,1)} %v_ref.1) | copy-start | bytes 3145732
  0.0 22.1 %copy-start.1 = (bf16[512,128]{1,0:T(8,128)(2,1)S(1)}, bf16[512,128]{1,0:T(8,128)(2,1)}, u32[]{:S(2)}) copy-start(bf16[512,128]{1,0:T(8,128)(2,1)} %kf_ref.1) | copy-start | bytes 393220
  0.0 22.1 %copy-start.3 = (bf16[512,128]{1,0:T(8,128)(2,1)S(1)}, bf16[512,128]{1,0:T(8,128)(2,1)}, u32[]{:S(2)}) copy-start(bf16[512,128]{1,0:T(8,128)(2,1)} %qf_ref.1) | copy-start | bytes 393220
  4.2 17.9 %copy-start.6 = (s32[8]{0:T(128)S(1)}, s32[8]{0:T(128)}, u32[]{:S(2)}) copy-start(s32[8]{0:T(128)} %get-tuple-element.29.n_ref) | copy-start | bytes 100
  4.2 14.0 %all-to-all-start = ((f32[4,320,128]{2,1,0:T(8,128)}), f32[4,320,128]{2,1,0:T(8,128)S(1)}, u32[]{:S(2)}, u32[]{:S(2)}) async-start(f32[4,320,128]{2,1,0:T(8,128)} %bitcast.16), calls=%async_computation | async-start | bytes 1310720 | tf_op jit(solution)/shard_map/all_to_all | solution.py:614
  8.2 24.4 %collective-permute-start.6 = (bf16[1024,128]{1,0:T(8,128)(2,1)}, bf16[1024,128]{1,0:T(8,128)(2,1)S(1)}, u32[]{:S(2)}, u32[]{:S(2)}) collective-permute-start(bf16[1024,128]{1,0:T(8,128)(2,1)} %get-tuple-element.42.own_hbm.refs_0_), channel_id=1, source_target_pairs={{0,192},{32,224},{1,193},{33,225},{2,194},{34,226},{3,195},{35,227... | collective-permute-start | bytes 786440 | tf_op jit(solution)/shard_map/ppermute | solution.py:617
  9.5 23.2 %collective-permute-start.5 = (bf16[1024,128]{1,0:T(8,128)(2,1)}, bf16[1024,128]{1,0:T(8,128)(2,1)S(1)}, u32[]{:S(2)}, u32[]{:S(2)}) collective-permute-start(bf16[1024,128]{1,0:T(8,128)(2,1)} %get-tuple-element.42.own_hbm.refs_0_), channel_id=1, source_target_pairs={{128,160},{160,192},{192,224},{129,161},{161,193},{193,225},{130,1... | collective-permute-start | bytes 786440 | tf_op jit(solution)/shard_map/ppermute | solution.py:616
  18.2 0.7 copy-start.5
  19.4 7.8 %collective-permute-start = (f32[320,128]{1,0:T(8,128)S(1)}, f32[320,128]{1,0:T(8,128)S(1)}, u32[]{:S(2)}, u32[]{:S(2)}) collective-permute-start(f32[320,128]{1,0:T(8,128)S(1)} %shard_map.75), channel_id=1, source_target_pairs={{0,32},{32,64},{64,96},{1,33},{33,65},{65,97},{2,34},{34,66},{66,9... | collective-permute-start | bytes 491528 | tf_op jit(solution)/shard_map/ppermute | solution.py:621
  20.7 8.3 %collective-permute-start.1 = (f32[320,128]{1,0:T(8,128)S(1)}, f32[320,128]{1,0:T(8,128)S(1)}, u32[]{:S(2)}, u32[]{:S(2)}) collective-permute-start(f32[320,128]{1,0:T(8,128)S(1)} %shard_map.75), channel_id=1, source_target_pairs={{128,64},{160,96},{0,192},{32,224},{129,65},{161,97},{1,193},{33,2... | collective-permute-start | bytes 491528 | tf_op jit(solution)/shard_map/ppermute | solution.py:622
  27.2 5.4 %copy-start.2 = (bf16[1024,128]{1,0:T(8,128)(2,1)S(1)}, bf16[1024,128]{1,0:T(8,128)(2,1)}, u32[]{:S(2)}) copy-start(bf16[1024,128]{1,0:T(8,128)(2,1)} %get-tuple-element.42.own_hbm.refs_0_) | copy-start | bytes 786436
  29.8 9.2 %collective-permute-start.2 = (f32[320,128]{1,0:T(8,128)S(1)}, f32[320,128]{1,0:T(8,128)S(1)}, u32[]{:S(2)}, u32[]{:S(2)}) collective-permute-start(f32[320,128]{1,0:T(8,128)S(1)} %get-tuple-element.37), channel_id=1, source_target_pairs={{0,8},{8,16},{16,24},{24,0},{1,9},{9,17},{17,25},{25,1},{2,10},{10... | collective-permute-start | bytes 491528 | tf_op jit(solution)/shard_map/ppermute | solution.py:603
  30.2 12.8 %collective-permute-start.3 = (f32[320,128]{1,0:T(8,128)S(1)}, f32[320,128]{1,0:T(8,128)S(1)}, u32[]{:S(2)}, u32[]{:S(2)}) collective-permute-start(f32[320,128]{1,0:T(8,128)S(1)} %get-tuple-element.38), channel_id=1, source_target_pairs={{0,16},{8,24},{16,0},{24,8},{1,17},{9,25},{17,1},{25,9},{2,18},{10... | collective-permute-start | bytes 491528 | tf_op jit(solution)/shard_map/ppermute | solution.py:603
  32.0 11.0 %collective-permute-start.4 = (f32[320,128]{1,0:T(8,128)S(1)}, f32[320,128]{1,0:T(8,128)S(1)}, u32[]{:S(2)}, u32[]{:S(2)}) collective-permute-start(f32[320,128]{1,0:T(8,128)S(1)} %get-tuple-element.39), channel_id=1, source_target_pairs={{0,24},{8,0},{16,8},{24,16},{1,25},{9,1},{17,9},{25,17},{2,26},{10... | collective-permute-start | bytes 491528 | tf_op jit(solution)/shard_map/ppermute | solution.py:603
  32.9 44.5 %collective-permute-start.7 = (bf16[2048,128]{1,0:T(8,128)(2,1)S(1)}, bf16[2048,128]{1,0:T(8,128)(2,1)S(1)}, u32[]{:S(2)}, u32[]{:S(2)}) collective-permute-start(bf16[2048,128]{1,0:T(8,128)(2,1)S(1)} %get-tuple-element.50), channel_id=1, source_target_pairs={{128,136},{136,144},{144,152},{152,128},{129,137},{137,145},{145,1... | collective-permute-start | bytes 1572872 | tf_op jit(solution)/shard_map/ppermute | solution.py:630
  35.6 41.8 %collective-permute-start.8 = (bf16[2048,128]{1,0:T(8,128)(2,1)S(1)}, bf16[2048,128]{1,0:T(8,128)(2,1)S(1)}, u32[]{:S(2)}, u32[]{:S(2)}) collective-permute-start(bf16[2048,128]{1,0:T(8,128)(2,1)S(1)} %get-tuple-element.51), channel_id=1, source_target_pairs={{128,144},{136,152},{144,128},{152,136},{129,145},{137,153},{145,1... | collective-permute-start | bytes 1572872 | tf_op jit(solution)/shard_map/ppermute | solution.py:630
  39.0 38.4 %collective-permute-start.9 = (bf16[2048,128]{1,0:T(8,128)(2,1)S(1)}, bf16[2048,128]{1,0:T(8,128)(2,1)S(1)}, u32[]{:S(2)}, u32[]{:S(2)}) collective-permute-start(bf16[2048,128]{1,0:T(8,128)(2,1)S(1)} %get-tuple-element.52), channel_id=1, source_target_pairs={{128,152},{136,128},{144,136},{152,144},{129,153},{137,129},{145,1... | collective-permute-start | bytes 1572872 | tf_op jit(solution)/shard_map/ppermute | solution.py:630
  43.0 16.7 %copy-start.4 = (f32[1024]{0:T(1024)S(1)}, f32[1024]{0:T(1024)}, u32[]{:S(2)}) copy-start(f32[1024]{0:T(1024)} %param.12) | copy-start | bytes 12292

commit v3 on v1

--- a/solution.py
+++ b/solution.py
@@ -17,6 +17,7 @@
 FEATS = 160
 QUARTER = HEADS * FEATS // 4
 SLOTS = 9
+DOC_ROW = USED + 2
 LOG2E = math.log2(math.e)
 FACTOR = LOG2E / math.sqrt(DH)
 SAFE = 110.0
@@ -64,37 +65,47 @@
     return lax.rem(x - s + 4, 4)
 
 
-def last_doc(block, n1, n2):
-    return doc_of(block * ROWS + ROWS - 1, n1, n2)
-
-
-def flag(x):
-    return x.astype(jnp.float32)
-
-
-def row_sum_kernel(n_ref, p0_ref, p1_ref, p2_ref, p3_ref, out_ref):
-    n1, n2 = n_ref[0], n_ref[1]
+def same(a, b):
+    return (a == b).astype(jnp.float32)
+
+
+def doc_row(ref):
+    return ref[DOC_ROW : DOC_ROW + 1, :]
+
+
+def row_sum_kernel(p0_ref, p1_ref, p2_ref, p3_ref, out_ref):
+    parts = (p0_ref, p1_ref, p2_ref, p3_ref)
+    end = doc_row(p0_ref)
+    for part in parts[1:]:
+        end = jnp.maximum(end, doc_row(part))
+    total = jnp.zeros((QUARTER, DH), jnp.float32)
+    for part in parts:
+        total = total + same(doc_row(part), end) * part[...]
+    out_ref[...] = total
+    out_ref[DOC_ROW : DOC_ROW + 1, :] = end
+
+
+def prior_kernel(p0_ref, p1_ref, p2_ref, p3_ref, near_ref, far_ref, *outs):
     z, x = here()
-    end = last_doc(z * 4 + 3, n1, n2)
-    total = jnp.zeros((QUARTER, DH), jnp.float32)
-    for s, part in enumerate((p0_ref, p1_ref, p2_ref, p3_ref)):
-        total = total + flag(last_doc(z * 4 + row_block(x, s), n1, n2) == end) * part[...]
-    out_ref[...] = total
-
-
-def prior_kernel(n_ref, p0_ref, p1_ref, p2_ref, p3_ref, near_ref, far_ref, *outs):
-    n1, n2 = n_ref[0], n_ref[1]
-    z, x = here()
-    before = last_doc(z * 4 - 1, n1, n2)
-    incoming = near_ref[...] + flag(last_doc(z * 4 - 5, n1, n2) == before) * far_ref[...]
+    parts = (p0_ref, p1_ref, p2_ref, p3_ref)
+    before = doc_row(near_ref)
+    incoming = near_ref[...] + same(doc_row(far_ref), before) * far_ref[...]
     for t, out in enumerate(outs):
         target = lax.rem(x + t, 4)
-        doc = last_doc(z * 4 + target - 1, n1, n2)
-        prior = flag(before == doc) * incoming
-        for s, part in enumerate((p0_ref, p1_ref, p2_ref, p3_ref)):
-            block = row_block(x, s)
-            prior = prior + flag((block < target) & (last_doc(z * 4 + block, n1, n2) == doc)) * part[...]
+        doc = before
+        for s, part in enumerate(parts):
+            doc = jnp.where(row_block(x, s) == target - 1, doc_row(part), doc)
+        prior = same(before, doc) * incoming
+        for s, part in enumerate(parts):
+            use = jnp.where(row_block(x, s) < target, same(doc_row(part), doc), 0.0)
+            prior = prior + use * part[...]
         out[...] = prior
+
+
+def stash_kernel(src_hbm, out_ref, sem):
+    copy = pltpu.make_async_copy(src_hbm, out_ref, sem)
+    copy.start()
+    copy.wait()
 
 
 def pack_kernel(own_hbm, near_hbm, far_hbm, o1_hbm, o2_hbm, o3_hbm, sems):
@@ -146,6 +157,8 @@
         base = h * FEATS + USED
         state_ref[base : base + 1, :] = across[h : h + 1, :DH]
         state_ref[base + 1 : base + 2, : FEATS - DH] = across[h : h + 1, DH:]
+        last = doc_of(first + ROWS - 1, n1, n2).astype(jnp.float32)
+        state_ref[base + 2 : base + 3, :] = jnp.full((1, DH), last, jnp.float32)
     for s, out in enumerate((c0_ref, c1_ref, c2_ref, c3_ref)):
         chunk = lax.rem(x + s, 4)
         out[...] = state_ref[pl.ds(pl.multiple_of(chunk * QUARTER, QUARTER), QUARTER), :]
@@ -249,18 +262,34 @@
     return jnp.max(lax.fori_loop(*slots, one, jnp.zeros((ROWS, 1), jnp.float32)))
 
 
-def make_queries(lin_ref, total_ref, gain_ref, q_ref):
-    scale = lax.rsqrt(total_ref[...] / ALL_WIDE + 1e-06)
-    scale = jnp.broadcast_to(scale, (DH, ROWS)).T
-    norm = jnp.zeros((ROWS, 1), jnp.float32)
-    for h in range(HEADS):
-        gain = gain_ref[0:1, h * DH : (h + 1) * DH]
-        q = (lin_ref[:, h * DH : (h + 1) * DH].astype(jnp.float32) * scale * gain).astype(jnp.bfloat16)
-        wide = q.astype(jnp.float32)
-        norm = jnp.maximum(norm, jnp.sum(wide * wide, 1, keepdims=True))
+def gauge_kernel(n_ref, lin_ref, gain_ref, near_ref, far_ref, rows_ref, stat_ref):
+    most = jnp.zeros((ROWS, 1), jnp.float32)
+    for h in range(HEADS):
+        lanes = slice(h * DH, (h + 1) * DH)
+        q = lin_ref[:, lanes].astype(jnp.float32) * gain_ref[0:1, lanes]
+        most = jnp.maximum(most, jnp.sum(q * q, 1, keepdims=True))
+    rows_ref[...] = jnp.broadcast_to(most, (ROWS, DH)).T[:8]
+    stat_ref[0] = 0.0
+    for slot, kv_ref in ((1, near_ref), (2, far_ref)):
+        k = kv_ref[:ROWS].astype(jnp.float32)
+        norm = jnp.max(jnp.sum(k * k, 1, keepdims=True))
+        stat_ref[0] = jnp.where(active(slot, n_ref[0], n_ref[1]), jnp.maximum(stat_ref[0], norm), stat_ref[0])
+
+
+def scale_of(total_ref):
+    return lax.rsqrt(total_ref[...] / ALL_WIDE + 1e-06)
+
+
+def make_queries(lin_ref, total_ref, gain_ref, q_ref, double):
+    scale = jnp.broadcast_to(scale_of(total_ref), (DH, ROWS)).T
+    for h in range(HEADS):
+        lanes = slice(h * DH, (h + 1) * DH)
+        q = (lin_ref[:, lanes].astype(jnp.float32) * scale * gain_ref[0:1, lanes]).astype(jnp.bfloat16)
+        lo = jnp.zeros((ROWS, DH), jnp.bfloat16)
+        if double:
+            q, lo = split(q.astype(jnp.float32) * FACTOR)
         q_ref[h, :, :DH] = q
-        q_ref[h, :, DH:] = jnp.zeros((ROWS, DH), jnp.bfloat16)
-    return jnp.max(norm)
+        q_ref[h, :, DH:] = lo
 
 
 def ones_beside(v):
@@ -311,7 +340,7 @@
     return first, first + lax.broadcasted_iota(jnp.int32, (ROWS, 1), 0)
 
 
-def open_kernel(n_ref, lin_ref, total_ref, gain_ref, near_hbm, far_hbm, q_ref, acc_ref, top_hbm, stat_ref, kv_ref, mask_ref, top_ref, sems):
+def open_kernel(n_ref, gauge_ref, lin_ref, total_ref, gain_ref, rows_ref, near_hbm, far_hbm, q_ref, acc_ref, top_hbm, stat_ref, kv_ref, mask_ref, top_ref, sems):
     @pl.when(in_softmax_phase())
     def _():
         n1, n2 = n_ref[0], n_ref[1]
@@ -319,20 +348,18 @@
         copies = [pltpu.make_async_copy(src, kv_ref.at[i], sems.at[i]) for i, src in enumerate((near_hbm, far_hbm))]
         for copy in copies:
             copy.start()
-        q_most = make_queries(lin_ref, total_ref, gain_ref, q_ref)
-        acc_ref[...] = jnp.zeros_like(acc_ref)
-        for copy in copies:
-            copy.wait()
-        safe = q_most * key_norms(kv_ref, (1, 3), 1, n1, n2) < (SAFE / FACTOR) ** 2
+        scale = scale_of(total_ref)
+        q_most = 1.02 * jnp.max(scale * scale * rows_ref[0:1, :])
+        safe = q_most * gauge_ref[0] < (SAFE / FACTOR) ** 2
         stat_ref[0] = q_most
         stat_ref[1] = jnp.where(safe, 1.0, 0.0)
+        acc_ref[...] = jnp.zeros_like(acc_ref)
 
         @pl.when(safe)
         def _():
-            for h in range(HEADS):
-                hi, lo = split(q_ref[h, :, :DH].astype(jnp.float32) * FACTOR)
-                q_ref[h, :, :DH] = hi
-                q_ref[h, :, DH:] = lo
+            make_queries(lin_ref, total_ref, gain_ref, q_ref, True)
+            for copy in copies:
+                copy.wait()
             begin_first = start_of(first, n1, n2)
 
             def step(slot, carry):
@@ -343,8 +370,11 @@
 
         @pl.when(jnp.logical_not(safe))
         def _():
+            make_queries(lin_ref, total_ref, gain_ref, q_ref, False)
             top_ref[...] = jnp.full(top_ref.shape, FAR, jnp.float32)
             begin = start_of(positions, n1, n2)
+            for copy in copies:
+                copy.wait()
 
             def step(slot, carry):
                 pl.when(active(slot, n1, n2))(
@@ -424,7 +454,7 @@
 
     @pl.when(jnp.logical_not(safe))
     def _():
-        make_queries(lin_ref, total_ref, gain_ref, raw_ref)
+        make_queries(lin_ref, total_ref, gain_ref, raw_ref, False)
 
         @pl.when(jnp.logical_not(opened_safe))
         def _():
@@ -480,20 +510,17 @@
     return jax.ShapeDtypeStruct(dims, dtype)
 
 
-def row_sum(counts, parts):
-    return call(row_sum_kernel, [shape((QUARTER, DH))], [VMEM], (counts,) + tuple(parts), [SMEM] + [VMEM] * 4, [], 0, 8)[0]
-
-
-def priors_of(counts, parts, near, far):
+def stash(chunk):
+    return call(stash_kernel, [shape(chunk.shape)], [VMEM], (chunk,), [ANY], [pltpu.SemaphoreType.DMA], 0, 4)[0]
+
+
+def row_sum(parts):
+    return call(row_sum_kernel, [shape((QUARTER, DH))], [VMEM], tuple(parts), [VMEM] * 4, [], 0, 8)[0]
+
+
+def priors_of(parts, near, far):
     return call(
-        prior_kernel,
-        [shape((QUARTER, DH))] * 4,
-        [VMEM] * 4,
-        (counts,) + tuple(parts) + (near, far),
-        [SMEM] + [VMEM] * 6,
-        [],
-        1000000000,
-        8,
+        prior_kernel, [shape((QUARTER, DH))] * 4, [VMEM] * 4, tuple(parts) + (near, far), [VMEM] * 6, [], 1000000000, 8
     )
 
 
@@ -557,14 +584,27 @@
     )
 
 
-def soft_open(counts, linear_out, total, gain, near_kv, far_kv):
+def gauge(counts, linear_out, gain, near_kv, far_kv):
+    return call(
+        gauge_kernel,
+        [shape((8, ROWS)), shape((8,))],
+        [VMEM, SMEM],
+        (counts, linear_out, gain, near_kv, far_kv),
+        [SMEM] + [VMEM] * 4,
+        [],
+        0,
+        8,
+    )
+
+
+def soft_open(counts, gauged, linear_out, total, gain, rows, near_kv, far_kv):
     bf16 = jnp.bfloat16
     return call(
         open_kernel,
         [shape((HEADS, ROWS, 256), bf16), shape((HEADS, ROWS, 256)), shape((HEADS, ROWS, DH)), shape((8,))],
         [VMEM, VMEM, ANY, SMEM],
-        (counts, linear_out, total, gain, near_kv, far_kv),
-        [SMEM] + [VMEM] * 3 + [ANY] * 2,
+        (counts, gauged, linear_out, total, gain, rows, near_kv, far_kv),
+        [SMEM] * 2 + [VMEM] * 4 + [ANY] * 2,
         [
             pltpu.VMEM((2, 2 * ROWS, DH), bf16),
             pltpu.VMEM((ROWS, ROWS), jnp.float32),
@@ -612,13 +652,13 @@
     zs = lax.axis_size("z")
     *chunks, own_kv, counts = states(doc_ids, key_feats, values, keys_soft, values_soft)
 
-    parts = [chunks[0]] + [shift(chunks[s], "x", s) for s in (1, 2, 3)]
+    parts = [stash(chunks[0])] + [shift(chunks[s], "x", s) for s in (1, 2, 3)]
 
     near_kv = lax.ppermute(own_kv, ("phase", "z"), [(zs + i, zs + i + 1) for i in range(zs - 1)])
     far_kv = lax.ppermute(own_kv, ("phase", "z"), [(i, zs + i + 2) for i in range(zs - 2)])
 
     local_sums = local_part(counts, query_feats, key_feats, values)
-    total = row_sum(counts, parts)
+    total = row_sum(parts)
     near = lax.ppermute(total, "z", [(i, i + 1) for i in range(zs - 1)])
     far = lax.ppermute(
         total,
@@ -633,15 +673,17 @@
     ]
 
     near = after(near, *local_sums)
-    priors = priors_of(counts, parts, near, far)
+    priors = priors_of(parts, near, far)
     arrived = [priors[0]] + [shift(priors[s], "x", s) for s in (1, 2, 3)]
     num, den, feats_hi, feats_lo = local_sums
     linear_out, squares = finish(counts, feats_hi, feats_lo, num, den, arrived)
     total = squares + shift(squares, "core", 1)
-    for pairs in ((1, 0, 3, 2), (3, 2, 1, 0)):
-        total = total + lax.ppermute(total, "y", list(enumerate(pairs)))
     gain = norm_gain[None]
-    queries, part, top, stat = soft_open(counts, linear_out, total, gain, near_kv, far_kv)
+    rows, gauged = gauge(counts, linear_out, gain, near_kv, far_kv)
+    total = total + lax.ppermute(total, "y", list(enumerate((1, 0, 3, 2))))
+    total = after(total, rows)
+    total = total + lax.ppermute(total, "y", list(enumerate((3, 2, 1, 0))))
+    queries, part, top, stat = soft_open(counts, gauged, linear_out, total, gain, rows, near_kv, far_kv)
     return soft_close(counts, stat, linear_out, total, gain, queries, part, top, [own_kv] + others)[None]
 
 

time: 118 us -> 114 us (0.966)
  the two profiles are of different devices: /device:TPU:230 before, /device:TPU:166 now
where the time goes in v3:
time: 114 us
  Pallas kernels  75.7 us (66%)
  starting transfers between devices  29.5 us (26%)
  waiting for transfers between devices  6.32 us (6%)
  local copies, waits for them, and re-layouts  1.55 us (1%)
    pallas_call x10, Pallas kernels, call(): pl.pallas_call(kernel, out_shape=tuple(outs), in_specs=in_specs, out_spec...  75.7 us
    ppermute x3, starting transfers between devices, local(): lax.ppermute(message, ('phase', 'x'), [(4 + i, 4 + (i + s) % 4) for i in...  10.3 us
    ppermute x7, starting transfers between devices, shift(): return lax.ppermute(x, axis, [(i, (i + by) % size) for i in range(size)])  6.3 us
    ppermute x7, waiting for transfers between devices, shift(): return lax.ppermute(x, axis, [(i, (i + by) % size) for i in range(size)])  4.27 us
    ppermute x1, starting transfers between devices, local(): lax.ppermute(own_kv, ('phase', 'z'), [(zs + i, zs + i + 1) for i in range...  3.55 us
    ppermute x1, starting transfers between devices, local(): near = lax.ppermute(total, 'z', [(i, i + 1) for i in range(zs - 1)])  2.92 us
    ppermute x1, starting transfers between devices, local(): total = total + lax.ppermute(total, 'y', list(enumerate((3, 2, 1, 0))))  2.85 us
  transfers between devices with their start and end apart: 16, of which 4 were waited for; matrix products, arithmetic and copies ran while one was open for 0% of the time, Pallas kernels for 18%

profile of v3, /device:TPU:166, one launch (start us, length us, event | category | flops | bytes accessed | tf_op | source)
XLA Modules:
  0.0 113.5 jit_solution(9381602570522453041)
XLA Ops:
  0.0 4.2 %shard_map.73 = (f32[320,128]{1,0:T(8,128)}, f32[320,128]{1,0:T(8,128)}, f32[320,128]{1,0:T(8,128)}, f32[320,128]{1,0:T(8,128)}, bf16[1024,128]{1,0:T(8,128)(2,1)}, /*index=5*/s32[8]{0:T(128)}) custom-call(s32[64,128]{1,0:T(8,128)} %bitcast.6, bf16[512,128]{1,0:T(8,128)(2,1)} %kf_ref.1, bf16[512,1024]{1,0:T(8,128)(2,1)} %v_ref.1, bf16[512,128]{1,0:T(8,128)(2,1)} %k_hbm.1, ...), custom_call_target="tpu_custom_call" | custom-call | tf_op jit(solution)/shard_map/pallas_call | solution.py:498
  4.8 2.4 %collective-permute-start.1 = (f32[320,128]{1,0:T(8,128)}, f32[320,128]{1,0:T(8,128)S(1)}, u32[]{:S(2)}, u32[]{:S(2)}) collective-permute-start(f32[320,128]{1,0:T(8,128)} %get-tuple-element.42), channel_id=1, source_target_pairs={{0,16},{8,24},{16,0},{24,8},{1,17},{9,25},{17,1},{25,9},{2,18},{10... | collective-permute-start | bytes 491528 | tf_op jit(solution)/shard_map/ppermute | solution.py:644
  7.2 0.7 collective-permute-start.9
  7.8 3.5 %collective-permute-start.8 = (bf16[1024,128]{1,0:T(8,128)(2,1)}, bf16[1024,128]{1,0:T(8,128)(2,1)S(1)}, u32[]{:S(2)}, u32[]{:S(2)}) collective-permute-start(bf16[1024,128]{1,0:T(8,128)(2,1)} %get-tuple-element.50.own_hbm.refs_0_), channel_id=1, source_target_pairs={{128,160},{160,192},{192,224},{129,161},{161,193},{193,225},{130,1... | collective-permute-start | bytes 786440 | tf_op jit(solution)/shard_map/ppermute | solution.py:657
  11.4 0.9 copy-done.3
  12.5 1.1 collective-permute-done.1.p2_ref
  13.6 2.0 %collective-permute-done.2.p3_ref = f32[320,128]{1,0:T(8,128)S(1)} collective-permute-done((f32[320,128]{1,0:T(8,128)}, f32[320,128]{1,0:T(8,128)S(1)}, u32[]{:S(2)}, u32[]{:S(2)}) %collective-permute-start.2) | collective-permute-done | bytes 163872 | tf_op jit(solution)/shard_map/ppermute | solution.py:644
  15.7 2.9 %collective-permute-start.3 = (f32[320,128]{1,0:T(8,128)S(1)}, f32[320,128]{1,0:T(8,128)S(1)}, u32[]{:S(2)}, u32[]{:S(2)}) collective-permute-start(f32[320,128]{1,0:T(8,128)S(1)} %shard_map.76), channel_id=1, source_target_pairs={{0,32},{32,64},{64,96},{1,33},{33,65},{65,97},{2,34},{34,66},{66,9... | collective-permute-start | bytes 491528 | tf_op jit(solution)/shard_map/ppermute | solution.py:662
  18.6 1.3 %collective-permute-start.4 = (f32[320,128]{1,0:T(8,128)S(1)}, f32[320,128]{1,0:T(8,128)S(1)}, u32[]{:S(2)}, u32[]{:S(2)}) collective-permute-start(f32[320,128]{1,0:T(8,128)S(1)} %shard_map.76), channel_id=1, source_target_pairs={{128,64},{160,96},{0,192},{32,224},{129,65},{161,97},{1,193},{33,2... | collective-permute-start | bytes 491528 | tf_op jit(solution)/shard_map/ppermute | solution.py:663
  20.0 0.6 copy-done.6
  20.6 5.0 %shard_map.74 = (f32[512,1024]{1,0:T(8,128)S(1)}, f32[512,128]{1,0:T(8,128)S(1)}, bf16[512,2048]{1,0:T(8,128)(2,1)S(1)}, bf16[512,2048]{1,0:T(8,128)(2,1)S(1)}) custom-call(s32[8]{0:T(128)S(1)} %copy-done.6, bf16[512,128]{1,0:T(8,128)(2,1)S(1)} %copy-done.4, bf16[512,128]{1,0:T(8,128)(2,1)S(1)} %copy-done.1, bf16[512,1024]{1,0:T(8,128)(2,1)S(1)} %copy-done), custom_call_target="tpu_custom_call" | custom-call | tf_op jit(solution)/shard_map/pallas_call | solution.py:498
  25.9 1.1 collective-permute-start.5
  27.0 2.1 %collective-permute-start.6 = (f32[320,128]{1,0:T(8,128)S(1)}, f32[320,128]{1,0:T(8,128)S(1)}, u32[]{:S(2)}, u32[]{:S(2)}) collective-permute-start(f32[320,128]{1,0:T(8,128)S(1)} %get-tuple-element.47), channel_id=1, source_target_pairs={{0,16},{8,24},{16,0},{24,8},{1,17},{9,25},{17,1},{25,9},{2,18},{10... | collective-permute-start | bytes 491528 | tf_op jit(solution)/shard_map/ppermute | solution.py:644
  29.4 5.0 %collective-permute-start.13 = (bf16[2048,128]{1,0:T(8,128)(2,1)S(1)}, bf16[2048,128]{1,0:T(8,128)(2,1)S(1)}, u32[]{:S(2)}, u32[]{:S(2)}) collective-permute-start(bf16[2048,128]{1,0:T(8,128)(2,1)S(1)} %get-tuple-element.62), channel_id=1, source_target_pairs={{128,136},{136,144},{144,152},{152,128},{129,137},{137,145},{145,1... | collective-permute-start | bytes 1572872 | tf_op jit(solution)/shard_map/ppermute | solution.py:671
  34.4 2.2 %collective-permute-start.14 = (bf16[2048,128]{1,0:T(8,128)(2,1)S(1)}, bf16[2048,128]{1,0:T(8,128)(2,1)S(1)}, u32[]{:S(2)}, u32[]{:S(2)}) collective-permute-start(bf16[2048,128]{1,0:T(8,128)(2,1)S(1)} %get-tuple-element.63), channel_id=1, source_target_pairs={{128,144},{136,152},{144,128},{152,136},{129,145},{137,153},{145,1... | collective-permute-start | bytes 1572872 | tf_op jit(solution)/shard_map/ppermute | solution.py:671
  36.6 3.1 %collective-permute-start.15 = (bf16[2048,128]{1,0:T(8,128)(2,1)S(1)}, bf16[2048,128]{1,0:T(8,128)(2,1)S(1)}, u32[]{:S(2)}, u32[]{:S(2)}) collective-permute-start(bf16[2048,128]{1,0:T(8,128)(2,1)S(1)} %get-tuple-element.64), channel_id=1, source_target_pairs={{128,152},{136,128},{144,136},{152,144},{129,153},{137,129},{145,1... | collective-permute-start | bytes 1572872 | tf_op jit(solution)/shard_map/ppermute | solution.py:671
  39.8 2.8 %shard_map.78 = (bf16[512,1024]{1,0:T(8,128)(2,1)S(1)}, f32[1,512]{1,0:T(1,128)S(1)}) custom-call(s32[8]{0:T(128)S(1)} %copy-done.7, bf16[512,2048]{1,0:T(8,128)(2,1)S(1)} %get-tuple-element.36.hi_ref, bf16[512,2048]{1,0:T(8,128)(2,1)S(1)} %get-tuple-element.37.lo_ref, f32[512,1024]{1,0:T(8,128)S(1)} %get-tuple-element.38.num_ref, ...), custom_call_target="tpu_custom_call" | custom-call | flops 8000000000 | tf_op jit(solution)/shard_map/pallas_call | solution.py:498
  42.7 1.1 %collective-permute-done.10 = f32[1,512]{1,0:T(1,128)S(1)} collective-permute-done((f32[1,512]{1,0:T(1,128)S(1)}, f32[1,512]{1,0:T(1,128)S(1)}, u32[]{:S(2)}, u32[]{:S(2)}) %collective-permute-start.10) | collective-permute-done | bytes 2080 | tf_op jit(solution)/shard_map/ppermute | solution.py:644
  43.9 1.6 %collective-permute-start.11 = (f32[1,512]{1,0:T(1,128)S(1)}, f32[1,512]{1,0:T(1,128)S(1)}, u32[]{:S(2)}, u32[]{:S(2)}) collective-permute-start(f32[1,512]{1,0:T(1,128)S(1)} %add.9), channel_id=1, source_target_pairs={{0,2},{2,0},{4,6},{6,4},{1,3},{3,1},{5,7},{7,5},{8,10},{10,8},{12,... | collective-permute-start | bytes 6152 | tf_op jit(solution)/shard_map/ppermute | solution.py:683
  45.5 2.2 %shard_map.79 = (f32[8,512]{1,0:T(8,128)S(1)}, f32[8]{0:T(128)S(1)}) custom-call(s32[8]{0:T(128)S(1)} %copy-done.7, bf16[512,1024]{1,0:T(8,128)(2,1)S(1)} %get-tuple-element.49.lin_ref, f32[1,1024]{1,0:T(1,128)S(1)} %bitcast.3, bf16[1024,128]{1,0:T(8,128)(2,1)S(1)} %collective-permute-done.8.near_ref.near_hbm, ...), custom_call_target="tpu_custom_call" | custom-call | tf_op jit(solution)/shard_map/pallas_call | solution.py:498
  47.6 2.8 %collective-permute-start.12 = (f32[1,512]{1,0:T(1,128)S(1)}, f32[1,512]{1,0:T(1,128)S(1)}, u32[]{:S(2)}, u32[]{:S(2)}) collective-permute-start(f32[1,512]{1,0:T(1,128)S(1)} %add.10), channel_id=1, source_target_pairs={{0,6},{2,4},{4,2},{6,0},{1,7},{3,5},{5,3},{7,1},{8,14},{10,12},{12... | collective-permute-start | bytes 6152 | tf_op jit(solution)/shard_map/ppermute | solution.py:685
  50.5 2.0 %collective-permute-done.12 = f32[1,512]{1,0:T(1,128)S(1)} collective-permute-done((f32[1,512]{1,0:T(1,128)S(1)}, f32[1,512]{1,0:T(1,128)S(1)}, u32[]{:S(2)}, u32[]{:S(2)}) %collective-permute-start.12) | collective-permute-done | bytes 2080 | tf_op jit(solution)/shard_map/ppermute | solution.py:685
  52.5 9.2 %shard_map.80 = (bf16[8,512,256]{2,1,0:T(8,128)(2,1)S(1)}, f32[8,512,256]{2,1,0:T(8,128)S(1)}, f32[8,512,128]{2,1,0:T(8,128)S(1)}, f32[8]{0:T(128)S(1)}) custom-call(s32[8]{0:T(128)S(1)} %copy-done.7, f32[8]{0:T(128)S(1)} %get-tuple-element.51.gauge_ref, bf16[512,1024]{1,0:T(8,128)(2,1)S(1)} %get-tuple-element.49.lin_ref, f32[1,512]{1,0:T(1,128)S(1)} %add.11.total_ref, ...), custom_call_target="tpu_custom_call" | custom-call | tf_op jit(solution)/shard_map/pallas_call | solution.py:498
  61.8 51.6 %shard_map.82 = bf16[512,1024]{1,0:T(8,128)(2,1)} custom-call(s32[8]{0:T(128)S(1)} %copy-done.7, f32[8]{0:T(128)S(1)} %get-tuple-element.55.stat_ref, bf16[512,1024]{1,0:T(8,128)(2,1)S(1)} %get-tuple-element.49.lin_ref, f32[1,512]{1,0:T(1,128)S(1)} %add.11.total_ref, f32[1,1024]{1,0:T(1,128)S(1)} %bitcast.5, ...), custom_call_target="tpu_custom_call" | custom-call | tf_op jit(solution)/shard_map/pallas_call | solution.py:498
  (37 shorter events, 1.5 us)
Async XLA Ops:
  0.0 19.9 %copy-start = (bf16[512,1024]{1,0:T(8,128)(2,1)S(1)}, bf16[512,1024]{1,0:T(8,128)(2,1)}, u32[]{:S(2)}) copy-start(bf16[512,1024]{1,0:T(8,128)(2,1)} %v_ref.1) | copy-start | bytes 3145732
  0.0 19.9 %copy-start.1 = (bf16[512,128]{1,0:T(8,128)(2,1)S(1)}, bf16[512,128]{1,0:T(8,128)(2,1)}, u32[]{:S(2)}) copy-start(bf16[512,128]{1,0:T(8,128)(2,1)} %kf_ref.1) | copy-start | bytes 393220
  0.0 19.9 %copy-start.4 = (bf16[512,128]{1,0:T(8,128)(2,1)S(1)}, bf16[512,128]{1,0:T(8,128)(2,1)}, u32[]{:S(2)}) copy-start(bf16[512,128]{1,0:T(8,128)(2,1)} %qf_ref.1) | copy-start | bytes 393220
  4.2 8.3 %collective-permute-start = (f32[320,128]{1,0:T(8,128)}, f32[320,128]{1,0:T(8,128)S(1)}, u32[]{:S(2)}, u32[]{:S(2)}) collective-permute-start(f32[320,128]{1,0:T(8,128)} %get-tuple-element.41), channel_id=1, source_target_pairs={{0,8},{8,16},{16,24},{24,0},{1,9},{9,17},{17,25},{25,1},{2,10},{10... | collective-permute-start | bytes 491528 | tf_op jit(solution)/shard_map/ppermute | solution.py:644
  4.8 8.8 %collective-permute-start.1 = (f32[320,128]{1,0:T(8,128)}, f32[320,128]{1,0:T(8,128)S(1)}, u32[]{:S(2)}, u32[]{:S(2)}) collective-permute-start(f32[320,128]{1,0:T(8,128)} %get-tuple-element.42), channel_id=1, source_target_pairs={{0,16},{8,24},{16,0},{24,8},{1,17},{9,25},{17,1},{25,9},{2,18},{10... | collective-permute-start | bytes 491528 | tf_op jit(solution)/shard_map/ppermute | solution.py:644
  7.2 8.5 %collective-permute-start.2 = (f32[320,128]{1,0:T(8,128)}, f32[320,128]{1,0:T(8,128)S(1)}, u32[]{:S(2)}, u32[]{:S(2)}) collective-permute-start(f32[320,128]{1,0:T(8,128)} %get-tuple-element.43), channel_id=1, source_target_pairs={{0,24},{8,0},{16,8},{24,16},{1,25},{9,1},{17,9},{25,17},{2,26},{10... | collective-permute-start | bytes 491528 | tf_op jit(solution)/shard_map/ppermute | solution.py:644
  7.2 22.0 %collective-permute-start.9 = (bf16[1024,128]{1,0:T(8,128)(2,1)}, bf16[1024,128]{1,0:T(8,128)(2,1)S(1)}, u32[]{:S(2)}, u32[]{:S(2)}) collective-permute-start(bf16[1024,128]{1,0:T(8,128)(2,1)} %get-tuple-element.50.own_hbm.refs_0_), channel_id=1, source_target_pairs={{0,192},{32,224},{1,193},{33,225},{2,194},{34,226},{3,195},{35,227... | collective-permute-start | bytes 786440 | tf_op jit(solution)/shard_map/ppermute | solution.py:658
  7.8 21.3 %collective-permute-start.8 = (bf16[1024,128]{1,0:T(8,128)(2,1)}, bf16[1024,128]{1,0:T(8,128)(2,1)S(1)}, u32[]{:S(2)}, u32[]{:S(2)}) collective-permute-start(bf16[1024,128]{1,0:T(8,128)(2,1)} %get-tuple-element.50.own_hbm.refs_0_), channel_id=1, source_target_pairs={{128,160},{160,192},{192,224},{129,161},{161,193},{193,225},{130,1... | collective-permute-start | bytes 786440 | tf_op jit(solution)/shard_map/ppermute | solution.py:657
  11.4 0.9 copy-start.3
  15.7 10.0 %collective-permute-start.3 = (f32[320,128]{1,0:T(8,128)S(1)}, f32[320,128]{1,0:T(8,128)S(1)}, u32[]{:S(2)}, u32[]{:S(2)}) collective-permute-start(f32[320,128]{1,0:T(8,128)S(1)} %shard_map.76), channel_id=1, source_target_pairs={{0,32},{32,64},{64,96},{1,33},{33,65},{65,97},{2,34},{34,66},{66,9... | collective-permute-start | bytes 491528 | tf_op jit(solution)/shard_map/ppermute | solution.py:662
  18.6 7.0 %collective-permute-start.4 = (f32[320,128]{1,0:T(8,128)S(1)}, f32[320,128]{1,0:T(8,128)S(1)}, u32[]{:S(2)}, u32[]{:S(2)}) collective-permute-start(f32[320,128]{1,0:T(8,128)S(1)} %shard_map.76), channel_id=1, source_target_pairs={{128,64},{160,96},{0,192},{32,224},{129,65},{161,97},{1,193},{33,2... | collective-permute-start | bytes 491528 | tf_op jit(solution)/shard_map/ppermute | solution.py:663
  20.0 0.6 copy-start.6
  25.6 3.5 %copy-start.2 = (bf16[1024,128]{1,0:T(8,128)(2,1)S(1)}, bf16[1024,128]{1,0:T(8,128)(2,1)}, u32[]{:S(2)}) copy-start(bf16[1024,128]{1,0:T(8,128)(2,1)} %get-tuple-element.50.own_hbm.refs_0_) | copy-start | bytes 786436
  25.9 10.7 %collective-permute-start.5 = (f32[320,128]{1,0:T(8,128)S(1)}, f32[320,128]{1,0:T(8,128)S(1)}, u32[]{:S(2)}, u32[]{:S(2)}) collective-permute-start(f32[320,128]{1,0:T(8,128)S(1)} %get-tuple-element.46), channel_id=1, source_target_pairs={{0,8},{8,16},{16,24},{24,0},{1,9},{9,17},{17,25},{25,1},{2,10},{10... | collective-permute-start | bytes 491528 | tf_op jit(solution)/shard_map/ppermute | solution.py:644
  27.0 12.8 %collective-permute-start.6 = (f32[320,128]{1,0:T(8,128)S(1)}, f32[320,128]{1,0:T(8,128)S(1)}, u32[]{:S(2)}, u32[]{:S(2)}) collective-permute-start(f32[320,128]{1,0:T(8,128)S(1)} %get-tuple-element.47), channel_id=1, source_target_pairs={{0,16},{8,24},{16,0},{24,8},{1,17},{9,25},{17,1},{25,9},{2,18},{10... | collective-permute-start | bytes 491528 | tf_op jit(solution)/shard_map/ppermute | solution.py:644
  29.0 10.7 %copy-start.7 = (s32[8]{0:T(128)S(1)}, s32[8]{0:T(128)}, u32[]{:S(2)}) copy-start(s32[8]{0:T(128)} %get-tuple-element.35.n_ref) | copy-start | bytes 100
  29.0 10.7 %collective-permute-start.7 = (f32[320,128]{1,0:T(8,128)S(1)}, f32[320,128]{1,0:T(8,128)S(1)}, u32[]{:S(2)}, u32[]{:S(2)}) collective-permute-start(f32[320,128]{1,0:T(8,128)S(1)} %get-tuple-element.48), channel_id=1, source_target_pairs={{0,24},{8,0},{16,8},{24,16},{1,25},{9,1},{17,9},{25,17},{2,26},{10... | collective-permute-start | bytes 491528 | tf_op jit(solution)/shard_map/ppermute | solution.py:644
  29.4 32.4 %collective-permute-start.13 = (bf16[2048,128]{1,0:T(8,128)(2,1)S(1)}, bf16[2048,128]{1,0:T(8,128)(2,1)S(1)}, u32[]{:S(2)}, u32[]{:S(2)}) collective-permute-start(bf16[2048,128]{1,0:T(8,128)(2,1)S(1)} %get-tuple-element.62), channel_id=1, source_target_pairs={{128,136},{136,144},{144,152},{152,128},{129,137},{137,145},{145,1... | collective-permute-start | bytes 1572872 | tf_op jit(solution)/shard_map/ppermute | solution.py:671
  34.4 27.4 %collective-permute-start.14 = (bf16[2048,128]{1,0:T(8,128)(2,1)S(1)}, bf16[2048,128]{1,0:T(8,128)(2,1)S(1)}, u32[]{:S(2)}, u32[]{:S(2)}) collective-permute-start(bf16[2048,128]{1,0:T(8,128)(2,1)S(1)} %get-tuple-element.63), channel_id=1, source_target_pairs={{128,144},{136,152},{144,128},{152,136},{129,145},{137,153},{145,1... | collective-permute-start | bytes 1572872 | tf_op jit(solution)/shard_map/ppermute | solution.py:671
  36.6 25.2 %collective-permute-start.15 = (bf16[2048,128]{1,0:T(8,128)(2,1)S(1)}, bf16[2048,128]{1,0:T(8,128)(2,1)S(1)}, u32[]{:S(2)}, u32[]{:S(2)}) collective-permute-start(bf16[2048,128]{1,0:T(8,128)(2,1)S(1)} %get-tuple-element.64), channel_id=1, source_target_pairs={{128,152},{136,128},{144,136},{152,144},{129,153},{137,129},{145,1... | collective-permute-start | bytes 1572872 | tf_op jit(solution)/shard_map/ppermute | solution.py:671
  39.8 5.7 %copy-start.5 = (f32[1024]{0:T(1024)S(1)}, f32[1024]{0:T(1024)}, u32[]{:S(2)}) copy-start(f32[1024]{0:T(1024)} %param.12) | copy-start | bytes 12292
  42.6 1.2 %collective-permute-start.10 = (f32[1,512]{1,0:T(1,128)S(1)}, f32[1,512]{1,0:T(1,128)S(1)}, u32[]{:S(2)}, u32[]{:S(2)}) collective-permute-start(f32[1,512]{1,0:T(1,128)S(1)} %get-tuple-element.52), channel_id=1, source_target_pairs={{0,1},{1,0},{2,3},{3,2},{4,5},{5,4},{6,7},{7,6},{8,9},{9,8},{10,11... | collective-permute-start | bytes 6152 | tf_op jit(solution)/shard_map/ppermute | solution.py:644
  43.9 3.7 %collective-permute-start.11 = (f32[1,512]{1,0:T(1,128)S(1)}, f32[1,512]{1,0:T(1,128)S(1)}, u32[]{:S(2)}, u32[]{:S(2)}) collective-permute-start(f32[1,512]{1,0:T(1,128)S(1)} %add.9), channel_id=1, source_target_pairs={{0,2},{2,0},{4,6},{6,4},{1,3},{3,1},{5,7},{7,5},{8,10},{10,8},{12,... | collective-permute-start | bytes 6152 | tf_op jit(solution)/shard_map/ppermute | solution.py:683
  47.6 4.9 %collective-permute-start.12 = (f32[1,512]{1,0:T(1,128)S(1)}, f32[1,512]{1,0:T(1,128)S(1)}, u32[]{:S(2)}, u32[]{:S(2)}) collective-permute-start(f32[1,512]{1,0:T(1,128)S(1)} %add.10), channel_id=1, source_target_pairs={{0,6},{2,4},{4,2},{6,0},{1,7},{3,5},{5,3},{7,1},{8,14},{10,12},{12... | collective-permute-start | bytes 6152 | tf_op jit(solution)/shard_map/ppermute | solution.py:685
